TPU v7x, 256 devices: a whole 4x4x8 slice. The times are simulated.
256 devices in a mesh: ta: 8 (over x, z_hi), tp: 32 (over y, z_lo, core).
Axes of the slice: x: 4, y: 4, z: 8 (z_hi: 2, z_lo: 4; z = z_hi * 4 + z_lo), core: 2. Of those that a mesh axis runs over, the one named last changes fastest.
Arguments:
- green: float32 [2, 8, 32, 16, 4096], P(None, None, 'tp', None, 'ta'), may hold values from -5 to 5
- hamiltonian: float32 [32, 32], replicated, may hold values from -1 to 1
- interaction: float32 [32, 32], replicated, may hold values from 0.4 to 1.2
Outputs:
- green_next: float32 [2, 8, 32, 16, 4096], P(None, None, 'tp', None, 'ta')
All inputs are finite; a program needn't handle non-finite values.
Results may differ from a plain program's by a relative error of at most 0.0091.
Values may be sent and summed in bfloat16 or wider, within the bound.
A program may use at most 64 MiB of HBM per device.

v0:
```python
import math

import jax
import jax.numpy as jnp
from jax import lax
from jax.sharding import PartitionSpec as P

NO = 32
ITERS = 2


highest = lax.Precision.HIGHEST


def shifted(block, axis, distance):
    devices = range(lax.axis_size(axis))
    route = [(i - distance, i) for i in devices if i - distance in devices]
    return lax.ppermute(block, axis, route)


def half_dot(left_side, right_side):
    return jnp.dot(left_side, right_side, preferred_element_type=jnp.float32)


def accumulate(left_side, right_side):
    product_real = half_dot(left_side[0], right_side[0]) - half_dot(left_side[1], right_side[1])
    product_imag = half_dot(left_side[0], right_side[1]) + half_dot(left_side[1], right_side[0])
    return (product_real, product_imag)


def self_energy(values, mirror_part, weights):
    real_square = values[0] * values[0] - values[1] * values[1]
    imag_square = 2.0 * values[0] * values[1]
    sigma_real = weights * (real_square * mirror_part[0] - imag_square * mirror_part[1])
    sigma_imag = weights * (real_square * mirror_part[1] + imag_square * mirror_part[0])
    return jnp.stack([sigma_real, sigma_imag])


def shards(green, hamiltonian, interaction):
    tp_count = lax.axis_size("tp")
    ta_place = lax.axis_index("ta")
    tp_place = lax.axis_index("tp")
    groups = green.shape[1]
    stripe = green.shape[3]
    block_rows = green.shape[4]
    columns = groups * stripe
    factor = 1.0 / math.sqrt(2 * block_rows)
    current = green[:, :, 0].reshape(2, columns, block_rows)
    squared = interaction * interaction
    column_global = (
        jnp.arange(groups, dtype=jnp.int32)[:, None] * tp_count + tp_place
    ) * stripe + jnp.arange(stripe, dtype=jnp.int32)[None, :]
    column_orbital = (column_global % NO).reshape(columns)
    onehot = (column_orbital[:, None] == jnp.arange(NO, dtype=jnp.int32)[None, :]).astype(
        jnp.float32
    )
    lookup_table = jnp.dot(onehot, squared.T, precision=highest)
    coupling = jnp.tile(lookup_table, (1, block_rows // NO))
    row_time = jnp.arange(block_rows, dtype=jnp.int32) // NO
    column_time = (tp_place * stripe + jnp.arange(stripe, dtype=jnp.int32)) // NO
    is_later = column_time[:, None] > row_time[None, :]
    block_width = math.gcd(block_rows, 128)
    blocked = jnp.kron(jnp.eye(block_width // NO, dtype=jnp.float32), hamiltonian.T)
    for iteration in range(ITERS):
        rounded = current.astype(jnp.bfloat16)
        outgoing = rounded.reshape(2, groups, stripe, tp_count, stripe)
        previous = shifted(rounded, "ta", 1)
        earliest = shifted(rounded, "ta", 2)
        hamilton_term = jnp.dot(
            current.reshape(-1, block_width), blocked, precision=highest
        ).reshape(2, columns, block_rows)
        selected = []
        nearby = jnp.stack(
            [
                lax.dynamic_index_in_dim(
                    outgoing, jnp.minimum(ta_place + step_ahead, groups - 1), 1, keepdims=False
                )
                for step_ahead in range(3)
            ],
            1,
        )
        spread = lax.all_to_all(nearby, "tp", split_axis=3, concat_axis=3, tiled=True)
        from_one = shifted(spread[:, 1], "ta", 1)
        from_two = shifted(spread[:, 2], "ta", 2)
        received = (from_two, from_one, spread[:, 0])
        by_current = current.reshape(2, groups, stripe, block_rows)
        for window_index in range(3):
            group_pick = jnp.maximum(ta_place - 2 + window_index, 0)
            own_part = lax.dynamic_index_in_dim(by_current, group_pick, 1, keepdims=False)
            flipped = (
                jnp.transpose(received[window_index], (0, 3, 2, 1))
                .reshape(2, stripe, block_rows)
                .astype(jnp.float32)
            )
            selected.append(self_energy(own_part, flipped, coupling[:stripe]))
        oldest = jnp.where(is_later[None], selected[0], 0.0)
        middle = selected[1]
        newest = jnp.where(is_later[None], 0.0, selected[2])
        sending = jnp.stack([oldest, middle, newest], 1).astype(jnp.bfloat16)[:, :, None]
        portion = lax.all_gather(sending, "tp", axis=2, tiled=True)
        row_count = portion.shape[2] * stripe
        right_side = jnp.concatenate(
            [portion[:, position].reshape(2, row_count, block_rows) for position in range(3)], 1
        )
        memory = accumulate(
            jnp.concatenate([source for source in (earliest, previous, rounded)], 2), right_side
        )
        next_real = current[0] + 0.5 * (hamilton_term[1] + factor * memory[1])
        next_imag = current[1] - 0.5 * (hamilton_term[0] + factor * memory[0])
        current = jnp.stack([next_real, next_imag])
    return current.reshape(2, groups, 1, stripe, block_rows)


def solution(mesh):
    in_specs = (P(None, None, "tp", None, "ta"), P(), P())
    out_specs = P(None, None, "tp", None, "ta")
    return jax.shard_map(shards, mesh=mesh, in_specs=in_specs, out_specs=out_specs, check_vma=False)
```

profile of v0, /device:TPU:1, one launch (start us, length us, event | category | flops | bytes accessed | tf_op | source)
XLA Modules:
  0.0 246.5 jit_solution(986032573024109374)
XLA Ops:
  6.5 1.1 convert_element_type.87
  7.6 1.7 convert_element_type.89
  9.9 1.3 reshape.846
  11.2 10.2 %all-to-all-start = ((bf16[32,2,768]{2,1,0:T(2,128)(2,1)}), bf16[32,2,768]{2,1,0:T(2,128)(2,1)S(1)}, u32[]{:S(2)}, u32[]{:S(2)}) async-start(bf16[32,2,768]{2,1,0:T(2,128)(2,1)} %reshape.846), calls=%async_computation | async-start | bytes 196608 | tf_op jit(solution)/shard_map/all_to_all | solution.py:82
  22.1 7.6 %all-to-all-done = bf16[32,2,768]{2,1,0:T(2,128)(2,1)S(1)} async-done(((bf16[32,2,768]{2,1,0:T(2,128)(2,1)}), bf16[32,2,768]{2,1,0:T(2,128)(2,1)S(1)}, u32[]{:S(2)}, u32[]{:S(2)}) %all-to-all-start) | async-done | bytes 98336 | tf_op jit(solution)/shard_map/all_to_all | solution.py:82
  30.4 3.1 %collective-permute-start.2 = (bf16[2,16,32,16]{3,1,0,2:T(8,128)(2,1)S(1)}, bf16[2,16,32,16]{3,1,0,2:T(8,128)(2,1)S(1)}, u32[]{:S(2)}, u32[]{:S(2)}) collective-permute-start(bf16[2,16,32,16]{3,1,0,2:T(8,128)(2,1)S(1)} %get-tuple-element.20), channel_id=1, source_target_pairs={{0,64},{32,96},{64,128},{96,160},{128,192},{160,224},{1,65},{33,97... | collective-permute-start | bytes 98312 | tf_op jit(solution)/shard_map/ppermute | solution.py:18
  33.8 6.1 %collective-permute-start.3 = (bf16[2,16,32,16]{3,1,0,2:T(8,128)(2,1)S(1)}, bf16[2,16,32,16]{3,1,0,2:T(8,128)(2,1)S(1)}, u32[]{:S(2)}, u32[]{:S(2)}) collective-permute-start(bf16[2,16,32,16]{3,1,0,2:T(8,128)(2,1)S(1)} %get-tuple-element.22), channel_id=1, source_target_pairs={{0,32},{32,64},{64,96},{96,128},{128,160},{160,192},{192,224},{1,3... | collective-permute-start | bytes 98312 | tf_op jit(solution)/shard_map/ppermute | solution.py:18
  40.2 11.0 %collective-permute-done.3 = bf16[2,16,32,16]{3,1,0,2:T(8,128)(2,1)S(1)} collective-permute-done((bf16[2,16,32,16]{3,1,0,2:T(8,128)(2,1)S(1)}, bf16[2,16,32,16]{3,1,0,2:T(8,128)(2,1)S(1)}, u32[]{:S(2)}, u32[]{:S(2)}) %collective-permute-start.3) | collective-permute-done | bytes 32800 | tf_op jit(solution)/shard_map/ppermute | solution.py:18
  52.4 5.2 %collective-permute-start = (bf16[2,128,512]{2,1,0:T(8,128)(2,1)S(1)}, bf16[2,128,512]{2,1,0:T(8,128)(2,1)S(1)}, u32[]{:S(2)}, u32[]{:S(2)}) collective-permute-start(bf16[2,128,512]{2,1,0:T(8,128)(2,1)S(1)} %bitcast.347), channel_id=1, source_target_pairs={{0,64},{32,96},{64,128},{96,160},{128,192},{160,224},{1,65},{33,97... | collective-permute-start | bytes 786440 | tf_op jit(solution)/shard_map/ppermute | solution.py:18
  57.6 5.7 %collective-permute-start.1 = (bf16[2,128,512]{2,1,0:T(8,128)(2,1)S(1)}, bf16[2,128,512]{2,1,0:T(8,128)(2,1)S(1)}, u32[]{:S(2)}, u32[]{:S(2)}) collective-permute-start(bf16[2,128,512]{2,1,0:T(8,128)(2,1)S(1)} %bitcast.348), channel_id=1, source_target_pairs={{0,32},{32,64},{64,96},{96,128},{128,160},{160,192},{192,224},{1,3... | collective-permute-start | bytes 786440 | tf_op jit(solution)/shard_map/ppermute | solution.py:18
  67.0 7.8 %collective-permute-done.1 = bf16[2,128,512]{2,1,0:T(8,128)(2,1)S(1)} collective-permute-done((bf16[2,128,512]{2,1,0:T(8,128)(2,1)S(1)}, bf16[2,128,512]{2,1,0:T(8,128)(2,1)S(1)}, u32[]{:S(2)}, u32[]{:S(2)}) %collective-permute-start.1) | collective-permute-done | bytes 262176 | tf_op jit(solution)/shard_map/ppermute | solution.py:18
  75.7 41.7 %all-gather.3.cloned.1.call-done = bf16[2,3,32,16,512]{4,3,0,2,1:T(8,128)(2,1)} async-done(((bf16[2,3,1,16,512]{4,3,0,2,1:T(8,128)(2,1)}), bf16[2,3,32,16,512]{4,3,0,2,1:T(8,128)(2,1)}) %all-gather.3.cloned.1.call-update) | async-done | bytes 3145744 | tf_op jit(solution)/shard_map/all_gather | solution.py:100
  117.5 2.2 fusion.85
  121.4 1.1 fusion
  123.5 2.7 %stack.132 = bf16[1,8,16,32,16]{4,3,2,1,0:T(8,128)(2,1)} reshape(bf16[128,512]{1,0:T(8,128)(2,1)} %get-tuple-element.62) | data formatting | bytes 262144 | tf_op jit(solution)/shard_map/stack | solution.py:110
  126.2 2.3 constant_dynamic-update-slice_fusion.1
  128.5 2.4 fusion.96
  130.8 1.8 stack.133
  132.7 1.1 constant_dynamic-update-slice_fusion
  133.8 1.2 constant_dynamic-slice_fusion.2
  135.5 1.3 reshape.848
  136.8 7.2 %all-to-all-start.1 = ((bf16[32,2,768]{2,1,0:T(2,128)(2,1)}), bf16[32,2,768]{2,1,0:T(2,128)(2,1)S(1)}, u32[]{:S(2)}, u32[]{:S(2)}) async-start(bf16[32,2,768]{2,1,0:T(2,128)(2,1)} %reshape.848), calls=%async_computation.1 | async-start | bytes 196608 | tf_op jit(solution)/shard_map/all_to_all | solution.py:82
  144.1 8.2 %all-to-all-done.1 = bf16[32,2,768]{2,1,0:T(2,128)(2,1)S(1)} async-done(((bf16[32,2,768]{2,1,0:T(2,128)(2,1)}), bf16[32,2,768]{2,1,0:T(2,128)(2,1)S(1)}, u32[]{:S(2)}, u32[]{:S(2)}) %all-to-all-start.1) | async-done | bytes 98336 | tf_op jit(solution)/shard_map/all_to_all | solution.py:82
  153.0 3.6 %collective-permute-start.7 = (bf16[2,16,32,16]{3,1,0,2:T(8,128)(2,1)S(1)}, bf16[2,16,32,16]{3,1,0,2:T(8,128)(2,1)S(1)}, u32[]{:S(2)}, u32[]{:S(2)}) collective-permute-start(bf16[2,16,32,16]{3,1,0,2:T(8,128)(2,1)S(1)} %get-tuple-element.19), channel_id=1, source_target_pairs={{0,32},{32,64},{64,96},{96,128},{128,160},{160,192},{192,224},{1,3... | collective-permute-start | bytes 98312 | tf_op jit(solution)/shard_map/ppermute | solution.py:18
  156.7 2.7 %collective-permute-start.6 = (bf16[2,16,32,16]{3,1,0,2:T(8,128)(2,1)S(1)}, bf16[2,16,32,16]{3,1,0,2:T(8,128)(2,1)S(1)}, u32[]{:S(2)}, u32[]{:S(2)}) collective-permute-start(bf16[2,16,32,16]{3,1,0,2:T(8,128)(2,1)S(1)} %get-tuple-element.17), channel_id=1, source_target_pairs={{0,64},{32,96},{64,128},{96,160},{128,192},{160,224},{1,65},{33,97... | collective-permute-start | bytes 98312 | tf_op jit(solution)/shard_map/ppermute | solution.py:18
  159.6 8.0 %collective-permute-done.7 = bf16[2,16,32,16]{3,1,0,2:T(8,128)(2,1)S(1)} collective-permute-done((bf16[2,16,32,16]{3,1,0,2:T(8,128)(2,1)S(1)}, bf16[2,16,32,16]{3,1,0,2:T(8,128)(2,1)S(1)}, u32[]{:S(2)}, u32[]{:S(2)}) %collective-permute-start.7) | collective-permute-done | bytes 32800 | tf_op jit(solution)/shard_map/ppermute | solution.py:18
  169.0 7.6 %collective-permute-start.4 = (bf16[2,128,512]{2,1,0:T(8,128)(2,1)S(1)}, bf16[2,128,512]{2,1,0:T(8,128)(2,1)S(1)}, u32[]{:S(2)}, u32[]{:S(2)}) collective-permute-start(bf16[2,128,512]{2,1,0:T(8,128)(2,1)S(1)} %fusion.83), channel_id=1, source_target_pairs={{0,64},{32,96},{64,128},{96,160},{128,192},{160,224},{1,65},{33,97... | collective-permute-start | bytes 786440 | tf_op jit(solution)/shard_map/ppermute | solution.py:18
  176.6 3.0 %collective-permute-start.5 = (bf16[2,128,512]{2,1,0:T(8,128)(2,1)S(1)}, bf16[2,128,512]{2,1,0:T(8,128)(2,1)S(1)}, u32[]{:S(2)}, u32[]{:S(2)}) collective-permute-start(bf16[2,128,512]{2,1,0:T(8,128)(2,1)S(1)} %fusion.83), channel_id=1, source_target_pairs={{0,32},{32,64},{64,96},{96,128},{128,160},{160,192},{192,224},{1,3... | collective-permute-start | bytes 786440 | tf_op jit(solution)/shard_map/ppermute | solution.py:18
  180.4 1.3 collective-permute-done.4
  181.8 11.4 %collective-permute-done.5 = bf16[2,128,512]{2,1,0:T(8,128)(2,1)S(1)} collective-permute-done((bf16[2,128,512]{2,1,0:T(8,128)(2,1)S(1)}, bf16[2,128,512]{2,1,0:T(8,128)(2,1)S(1)}, u32[]{:S(2)}, u32[]{:S(2)}) %collective-permute-start.5) | collective-permute-done | bytes 262176 | tf_op jit(solution)/shard_map/ppermute | solution.py:18
  193.2 41.4 %all-gather.5.cloned.1.call-done = bf16[2,3,32,16,512]{4,3,0,2,1:T(8,128)(2,1)} async-done(((bf16[2,3,1,16,512]{4,3,0,2,1:T(8,128)(2,1)}), bf16[2,3,32,16,512]{4,3,0,2,1:T(8,128)(2,1)}) %all-gather.5.cloned.1.call-update) | async-done | bytes 3145744 | tf_op jit(solution)/shard_map/all_gather | solution.py:100
  234.6 2.2 fusion.84
  (110 shorter events, 17.4 us)
Async XLA Ops:
  9.3 12.3 %copy-start.6 = (f32[32,32]{1,0:T(8,128)S(1)}, f32[32,32]{1,0:T(8,128)}, u32[]{:S(2)}) copy-start(f32[32,32]{1,0:T(8,128)} %param.5) | copy-start | bytes 12292
  11.2 18.5 %all-to-all-start = ((bf16[32,2,768]{2,1,0:T(2,128)(2,1)}), bf16[32,2,768]{2,1,0:T(2,128)(2,1)S(1)}, u32[]{:S(2)}, u32[]{:S(2)}) async-start(bf16[32,2,768]{2,1,0:T(2,128)(2,1)} %reshape.846), calls=%async_computation | async-start | bytes 196608 | tf_op jit(solution)/shard_map/all_to_all | solution.py:82
  21.4 96.1 %all-gather.3.cloned.1.call-start = ((), (), s32[]{:S(2)}) async-start(), calls=%async_computation.2 | async-start | bytes 3244032 | tf_op jit(solution)/shard_map/all_gather | solution.py:100
  30.4 9.5 %collective-permute-start.2 = (bf16[2,16,32,16]{3,1,0,2:T(8,128)(2,1)S(1)}, bf16[2,16,32,16]{3,1,0,2:T(8,128)(2,1)S(1)}, u32[]{:S(2)}, u32[]{:S(2)}) collective-permute-start(bf16[2,16,32,16]{3,1,0,2:T(8,128)(2,1)S(1)} %get-tuple-element.20), channel_id=1, source_target_pairs={{0,64},{32,96},{64,128},{96,160},{128,192},{160,224},{1,65},{33,97... | collective-permute-start | bytes 98312 | tf_op jit(solution)/shard_map/ppermute | solution.py:18
  33.5 18.0 %copy-start.1 = (f32[2,8,1,16,512]{4,3,2,1,0:T(8,128)S(1)}, f32[2,8,1,16,512]{4,3,2,1,0:T(8,128)}, u32[]{:S(2)}) copy-start(f32[2,8,1,16,512]{4,3,2,1,0:T(8,128)} %param.3) | copy-start | bytes 1572868
  33.8 17.5 %collective-permute-start.3 = (bf16[2,16,32,16]{3,1,0,2:T(8,128)(2,1)S(1)}, bf16[2,16,32,16]{3,1,0,2:T(8,128)(2,1)S(1)}, u32[]{:S(2)}, u32[]{:S(2)}) collective-permute-start(bf16[2,16,32,16]{3,1,0,2:T(8,128)(2,1)S(1)} %get-tuple-element.22), channel_id=1, source_target_pairs={{0,32},{32,64},{64,96},{96,128},{128,160},{160,192},{192,224},{1,3... | collective-permute-start | bytes 98312 | tf_op jit(solution)/shard_map/ppermute | solution.py:18
  40.0 23.3 %copy-start.5 = (f32[32,32]{1,0:T(8,128)S(1)}, f32[32,32]{1,0:T(8,128)}, u32[]{:S(2)}) copy-start(f32[32,32]{1,0:T(8,128)} %param.4) | copy-start | bytes 12292
  52.4 14.6 %collective-permute-start = (bf16[2,128,512]{2,1,0:T(8,128)(2,1)S(1)}, bf16[2,128,512]{2,1,0:T(8,128)(2,1)S(1)}, u32[]{:S(2)}, u32[]{:S(2)}) collective-permute-start(bf16[2,128,512]{2,1,0:T(8,128)(2,1)S(1)} %bitcast.347), channel_id=1, source_target_pairs={{0,64},{32,96},{64,128},{96,160},{128,192},{160,224},{1,65},{33,97... | collective-permute-start | bytes 786440 | tf_op jit(solution)/shard_map/ppermute | solution.py:18
  57.6 17.2 %collective-permute-start.1 = (bf16[2,128,512]{2,1,0:T(8,128)(2,1)S(1)}, bf16[2,128,512]{2,1,0:T(8,128)(2,1)S(1)}, u32[]{:S(2)}, u32[]{:S(2)}) collective-permute-start(bf16[2,128,512]{2,1,0:T(8,128)(2,1)S(1)} %bitcast.348), channel_id=1, source_target_pairs={{0,32},{32,64},{64,96},{96,128},{128,160},{160,192},{192,224},{1,3... | collective-permute-start | bytes 786440 | tf_op jit(solution)/shard_map/ppermute | solution.py:18
  119.9 1.1 copy-start.2
  121.0 1.4 copy-start.3
  121.0 1.4 copy-start.4
  133.8 10.3 %copy-start = (f32[128,512]{1,0:T(8,128)S(1)}, f32[128,512]{1,0:T(8,128)}, u32[]{:S(2)}) copy-start(f32[128,512]{1,0:T(8,128)} %get-tuple-element.65) | copy-start | bytes 786436
  136.8 15.5 %all-to-all-start.1 = ((bf16[32,2,768]{2,1,0:T(2,128)(2,1)}), bf16[32,2,768]{2,1,0:T(2,128)(2,1)S(1)}, u32[]{:S(2)}, u32[]{:S(2)}) async-start(bf16[32,2,768]{2,1,0:T(2,128)(2,1)} %reshape.848), calls=%async_computation.1 | async-start | bytes 196608 | tf_op jit(solution)/shard_map/all_to_all | solution.py:82
  144.1 90.5 %all-gather.5.cloned.1.call-start = ((), (), s32[]{:S(2)}) async-start(), calls=%async_computation.3 | async-start | bytes 3244032 | tf_op jit(solution)/shard_map/all_gather | solution.py:100
  153.0 14.5 %collective-permute-start.7 = (bf16[2,16,32,16]{3,1,0,2:T(8,128)(2,1)S(1)}, bf16[2,16,32,16]{3,1,0,2:T(8,128)(2,1)S(1)}, u32[]{:S(2)}, u32[]{:S(2)}) collective-permute-start(bf16[2,16,32,16]{3,1,0,2:T(8,128)(2,1)S(1)} %get-tuple-element.19), channel_id=1, source_target_pairs={{0,32},{32,64},{64,96},{96,128},{128,160},{160,192},{192,224},{1,3... | collective-permute-start | bytes 98312 | tf_op jit(solution)/shard_map/ppermute | solution.py:18
  156.7 11.2 %collective-permute-start.6 = (bf16[2,16,32,16]{3,1,0,2:T(8,128)(2,1)S(1)}, bf16[2,16,32,16]{3,1,0,2:T(8,128)(2,1)S(1)}, u32[]{:S(2)}, u32[]{:S(2)}) collective-permute-start(bf16[2,16,32,16]{3,1,0,2:T(8,128)(2,1)S(1)} %get-tuple-element.17), channel_id=1, source_target_pairs={{0,64},{32,96},{64,128},{96,160},{128,192},{160,224},{1,65},{33,97... | collective-permute-start | bytes 98312 | tf_op jit(solution)/shard_map/ppermute | solution.py:18
  169.0 12.7 %collective-permute-start.4 = (bf16[2,128,512]{2,1,0:T(8,128)(2,1)S(1)}, bf16[2,128,512]{2,1,0:T(8,128)(2,1)S(1)}, u32[]{:S(2)}, u32[]{:S(2)}) collective-permute-start(bf16[2,128,512]{2,1,0:T(8,128)(2,1)S(1)} %fusion.83), channel_id=1, source_target_pairs={{0,64},{32,96},{64,128},{96,160},{128,192},{160,224},{1,65},{33,97... | collective-permute-start | bytes 786440 | tf_op jit(solution)/shard_map/ppermute | solution.py:18
  176.6 16.5 %collective-permute-start.5 = (bf16[2,128,512]{2,1,0:T(8,128)(2,1)S(1)}, bf16[2,128,512]{2,1,0:T(8,128)(2,1)S(1)}, u32[]{:S(2)}, u32[]{:S(2)}) collective-permute-start(bf16[2,128,512]{2,1,0:T(8,128)(2,1)S(1)} %fusion.83), channel_id=1, source_target_pairs={{0,32},{32,64},{64,96},{96,128},{128,160},{160,192},{192,224},{1,3... | collective-permute-start | bytes 786440 | tf_op jit(solution)/shard_map/ppermute | solution.py:18
Sparse Core Ops, SparseCore 0:
  52.5 64.9 all-gather.2
  169.1 65.4 all-gather.4
where the time goes:
time: 248 us; the launch traced here: 246 us
  waiting for transfers between devices  138 us (56%)
  starting transfers between devices  54.5 us (22%)
  local copies, waits for them, and re-layouts  25.5 us (10%)
  between operations  14.1 us (6%)
  matrix products  7.75 us (3%)
  other arithmetic  6.17 us (2%)
    all_gather x2, waiting for transfers between devices, shards(): portion = lax.all_gather(sending, 'tp', axis=2, tiled=True)  83.1 us
    ppermute x8, waiting for transfers between devices, shifted(): return lax.ppermute(block, axis, route)  39.5 us
    ppermute x8, starting transfers between devices, shifted(): return lax.ppermute(block, axis, route)  37 us
    all_to_all x2, starting transfers between devices, shards(): lax.all_to_all(nearby, 'tp', split_axis=3, concat_axis=3, tiled=True)  17.4 us
    all_to_all x2, waiting for transfers between devices, shards(): lax.all_to_all(nearby, 'tp', split_axis=3, concat_axis=3, tiled=True)  15.8 us
    unnamed x19, local copies, waits for them, and re-layouts  6.88 us
    dot_general x8, matrix products, half_dot(): return jnp.dot(left_side, right_side, preferred_element_type=jnp.float32)  6.35 us
    another operation x3, local copies, waits for them, and re-layouts, shards(): current = jnp.stack([next_real, next_imag])  5.62 us
  transfers between devices with their start and end apart: 12, of which 9 were waited for; matrix products, arithmetic and copies ran while one was open for 3% of the time, Pallas kernels for 0%

commit v1 on v0

v1 whole, which is shorter than its diff:
```python
import functools

import jax
import jax.numpy as jnp
from jax import lax
from jax.experimental import pallas as pl
from jax.experimental.pallas import tpu as pltpu
from jax.sharding import PartitionSpec as P

NO = 32
ITERS = 2
N_TA = 8
N_TP = 32
N_Y = 4
N_Z = 4
STRIPE = 16
ROWS = 512
COLS = 128
FACTOR = 1.0 / 32.0

MESH = pl.DeviceIdType.MESH
HIGHEST = lax.Precision.HIGHEST
F32 = jnp.float32
BF16 = jnp.bfloat16


def iota(shape, dim):
    return lax.broadcasted_iota(jnp.int32, shape, dim)


def exact_dot(left, right, contract=((1,), (0,))):
    return lax.dot_general(
        left, right, (contract, ((), ())), precision=HIGHEST, preferred_element_type=F32
    )


def kernel(
    green_ref,
    ham_ref,
    inter_ref,
    out_ref,
    rounded,
    previous,
    earliest,
    mirror_out,
    mirror_in,
    flip_own,
    flip_out,
    flip_in,
    window,
    straight,
    crossed,
    total,
    hamilton,
    weights,
    blocked,
    row_send,
    row_recv,
    mirror_send,
    mirror_recv,
    flip_send,
    flip_recv,
    window_send,
    window_recv,
):
    ta = lax.axis_index("ta")
    tp = lax.axis_index("tp")
    y = tp // 8
    zl = lax.rem(tp // 2, 4)
    core = lax.rem(tp, 2)

    def ta_plus(k):
        return lax.rem(ta + k + N_TA, N_TA)

    def place(dy, z, c):
        return lax.rem(y + dy, N_Y) * 8 + z * 2 + c

    barrier = pltpu.get_barrier_semaphore()

    def greet(k, carry):
        pl.semaphore_signal(
            barrier, inc=1, device_id=(ta, lax.rem(tp + k, N_TP)), device_id_type=MESH
        )
        return carry

    lax.fori_loop(1, N_TP, greet, 0)
    for k in (1, 2):
        pl.semaphore_signal(
            barrier, inc=1, device_id=(ta_plus(-k), tp), device_id_type=MESH
        )

    def remote(src, dst, send, recv, target):
        return pltpu.make_async_remote_copy(
            src_ref=src,
            dst_ref=dst,
            send_sem=send,
            recv_sem=recv,
            device_id=target,
            device_id_type=MESH,
        )

    def build_mirror(state, it):
        pieces = []
        for k in range(3):
            group = pl.multiple_of(ta_plus(k) * STRIPE, STRIPE)
            for r in range(2):
                pieces.append(state[r, pl.ds(group, STRIPE), :])
        pieces.append(jnp.zeros((2 * STRIPE, ROWS), F32))
        stacked = jnp.concatenate(pieces, axis=0)
        mirror_out[it] = stacked.T.astype(BF16)

    def build_rounded(state, it):
        for r in range(2):
            rounded[it, pl.ds(r * COLS, COLS), :] = state[r].astype(BF16)

    def row_copy(it, k):
        return remote(
            rounded.at[it],
            (previous if k == 1 else earliest).at[it],
            row_send.at[it, k - 1],
            row_recv.at[it, k - 1],
            (ta_plus(k), tp),
        )

    def flip_copy(it, k):
        return remote(
            flip_out.at[it, k - 1],
            flip_in.at[it, k - 1],
            flip_send.at[it, k - 1],
            flip_recv.at[it, k - 1],
            (ta_plus(k), tp),
        )

    def send_mirror(it):
        def send(k, carry):
            peer = lax.rem(tp + k, N_TP)
            remote(
                mirror_out.at[it, pl.ds(pl.multiple_of(peer * STRIPE, STRIPE), STRIPE), :],
                mirror_in.at[it, pl.ds(pl.multiple_of(tp * STRIPE, STRIPE), STRIPE), :],
                mirror_send.at[it],
                mirror_recv.at[it],
                (ta, peer),
            ).start()
            return carry

        lax.fori_loop(1, N_TP, send, 0)
        own = pl.ds(pl.multiple_of(tp * STRIPE, STRIPE), STRIPE)
        mirror_in[it, own, :] = mirror_out[it, own, :]

    def wait_bytes(ref, sem):
        pltpu.make_async_copy(ref, ref, sem).wait()

    def flip(it):
        piece = iota((STRIPE, 128), 1) // STRIPE
        for j in range(4):
            parts = [
                mirror_in[it, pl.ds((j * 8 + i) * STRIPE, STRIPE), :].astype(F32)
                for i in range(8)
            ]
            for bit in (1, 2, 4):
                low = (piece // bit) % 2 == 0
                for i in range(8):
                    if i & bit:
                        continue
                    first, second = parts[i], parts[i | bit]
                    parts[i] = jnp.where(low, first, pltpu.roll(second, STRIPE * bit, 1))
                    parts[i | bit] = jnp.where(
                        low, pltpu.roll(first, 128 - STRIPE * bit, 1), second
                    )
            for k in range(3):
                both = jnp.concatenate([parts[2 * k], parts[2 * k + 1]], axis=0).astype(BF16)
                lanes = pl.ds(j * 128, 128)
                if k == 0:
                    flip_own[:, lanes] = both
                else:
                    flip_out[it, k - 1, :, lanes] = both

    def column(state, r, k):
        group = pl.multiple_of(ta_plus(-k) * STRIPE, STRIPE)
        return state[r, pl.ds(group, STRIPE), :]

    def self_energy(it, kind, real, imag, mirror_real, mirror_imag):
        real_square = real * real - imag * imag
        imag_square = 2.0 * real * imag
        coupling = weights[...]
        own = pl.ds(pl.multiple_of(tp * STRIPE, STRIPE), STRIPE)
        window[it, 2 * kind, own, :] = (
            coupling * (real_square * mirror_real - imag_square * mirror_imag)
        ).astype(BF16)
        window[it, 2 * kind + 1, own, :] = (
            coupling * (real_square * mirror_imag + imag_square * mirror_real)
        ).astype(BF16)

    def sigma_combined(state, it):
        later = iota((STRIPE, ROWS), 1) // NO < tp // 2
        real, imag = (
            jnp.where(later, column(state, r, 2), column(state, r, 0)) for r in range(2)
        )
        mirror_real, mirror_imag = (
            jnp.where(
                later,
                flip_in[it, 1, pl.ds(r * STRIPE, STRIPE), :].astype(F32),
                flip_own[pl.ds(r * STRIPE, STRIPE), :].astype(F32),
            )
            for r in range(2)
        )
        self_energy(it, 0, real, imag, mirror_real, mirror_imag)

    def sigma_middle(state, it):
        mirror_real, mirror_imag = (
            flip_in[it, 0, pl.ds(r * STRIPE, STRIPE), :].astype(F32) for r in range(2)
        )
        self_energy(
            it, 1, column(state, 0, 1), column(state, 1, 1), mirror_real, mirror_imag
        )

    def block(it, q):
        return window.at[it, :, pl.ds(pl.multiple_of(q * STRIPE, STRIPE), STRIPE), :]

    def send_block(it, q, target):
        remote(
            block(it, q), block(it, q), window_send.at[it], window_recv.at[it, q], (ta, target)
        ).start()

    def wait_block(it, q):
        wait_bytes(block(it, q), window_recv.at[it, q])

    near = zl + 1 - 2 * lax.rem(zl, 2)
    middle = 2 - zl // 2
    far = 3 * (1 - zl // 2)
    z_order = (zl, near, middle, far)

    def send_y(it, q):
        for dy in (1, 3, 2):
            send_block(it, q, lax.rem(tp + 8 * dy, N_TP))
        send_block(it, q, tp + 1 - 2 * core)

    def lefts(it, which, source, keep):
        for r in range(2):
            half = source[it, pl.ds(r * COLS, COLS), :]
            if keep is not None:
                half = jnp.where(keep, half, jnp.zeros_like(half))
            straight[which, pl.ds(r * COLS, COLS), :] = half
            crossed[which, pl.ds((1 - r) * COLS, COLS), :] = -half if r == 1 else half

    def multiply(it, dy):
        j = lax.rem(y + dy, N_Y)
        lanes = pl.ds(pl.multiple_of(j * 128, 128), 128)
        later = (j * 4 + iota((128, ROWS), 0) // NO) > iota((128, ROWS), 1) // NO
        old = jnp.where(later, 1.0, 0.0).astype(BF16)
        new = jnp.where(later, 0.0, 1.0).astype(BF16)
        left_parts, right_parts = [], []
        for r, side in ((0, straight), (1, crossed)):
            combined = window[it, r, lanes, :]
            right_parts += [combined * new, combined * old, window[it, 2 + r, lanes, :]]
            left_parts += [side[which, :, lanes] for which in range(3)]
        product = jnp.dot(
            jnp.concatenate(left_parts, axis=1),
            jnp.concatenate(right_parts, axis=0),
            preferred_element_type=F32,
        )
        if dy == 0:
            total[...] = product
        else:
            total[...] += product

    def hamilton_term(state):
        for r in range(2):
            for b in range(4):
                lanes = pl.ds(b * 128, 128)
                hamilton[pl.ds(r * COLS, COLS), lanes] = exact_dot(
                    state[r, :, lanes], blocked[...]
                )

    def prepare():
        squared = inter_ref[...] * inter_ref[...]
        pick = (iota((STRIPE, NO), 1) == core * STRIPE + iota((STRIPE, NO), 0)).astype(F32)
        picked = exact_dot(pick, squared, ((1,), (1,)))
        spread = (lax.rem(iota((NO, ROWS), 1), NO) == iota((NO, ROWS), 0)).astype(F32)
        weights[...] = exact_dot(picked, spread)
        tall = (lax.rem(iota((128, NO), 0), NO) == iota((128, NO), 1)).astype(F32)
        wide = (lax.rem(iota((NO, 128), 1), NO) == iota((NO, 128), 0)).astype(F32)
        across = exact_dot(exact_dot(tall, ham_ref[...], ((1,), (1,))), wide)
        same = iota((128, 128), 0) // NO == iota((128, 128), 1) // NO
        blocked[...] = jnp.where(same, across, 0.0)

    build_mirror(green_ref, 0)
    build_rounded(green_ref, 0)
    pl.semaphore_wait(barrier, N_TP - 1 + 2)

    for it in range(ITERS):
        state = green_ref if it == 0 else out_ref
        if it:
            build_mirror(state, it)
            build_rounded(state, it)
        send_mirror(it)
        rows = [row_copy(it, 2), row_copy(it, 1)]
        for copy in rows:
            copy.start()
        if it == 0:
            prepare()
        lefts(it, 0, rounded, None)
        wait_bytes(mirror_in.at[it, pl.ds(0, 31 * STRIPE), :], mirror_recv.at[it])
        flip(it)
        flips = [flip_copy(it, 1), flip_copy(it, 2)]
        for copy in flips:
            copy.start()
        hamilton_term(state)
        flips[1].wait_recv()
        sigma_combined(state, it)
        flips[0].wait_recv()
        sigma_middle(state, it)
        for z in (near, middle, far):
            send_block(it, tp, place(0, z, core))
        send_y(it, tp)
        for z in (near, middle, far):
            q = place(0, z, core)
            wait_block(it, q)
            send_y(it, q)
        rows[0].wait_recv()
        lefts(it, 2 - 1, earliest, ta >= 2)
        rows[1].wait_recv()
        lefts(it, 2, previous, ta >= 1)
        for z in z_order:
            wait_block(it, place(0, z, 1 - core))
        multiply(it, 0)
        for z in z_order:
            for dy in (1, 3, 2):
                q = place(dy, z, core)
                wait_block(it, q)
                send_block(it, q, tp + 1 - 2 * core)
        for dy in (1, 3, 2):
            for z in z_order:
                wait_block(it, place(dy, z, 1 - core))
            multiply(it, dy)
        out_real = state[0] + 0.5 * (
            hamilton[pl.ds(COLS, COLS), :] + FACTOR * total[pl.ds(COLS, COLS), :]
        )
        out_imag = state[1] - 0.5 * (
            hamilton[pl.ds(0, COLS), :] + FACTOR * total[pl.ds(0, COLS), :]
        )
        out_ref[0] = out_real
        out_ref[1] = out_imag
        wait_bytes(mirror_out.at[it, pl.ds(0, 31 * STRIPE), :], mirror_send.at[it])
        for copy in rows + flips:
            copy.wait_send()
        wait_bytes(window.at[it, :, pl.ds(0, 31 * STRIPE), :], window_send.at[it])


def shards(green, hamiltonian, interaction):
    shape = green.shape
    whole = pl.BlockSpec(memory_space=pltpu.VMEM)
    dma = pltpu.SemaphoreType.DMA
    result = pl.pallas_call(
        kernel,
        out_shape=jax.ShapeDtypeStruct((2, COLS, ROWS), F32),
        in_specs=[whole] * 3,
        out_specs=whole,
        scratch_shapes=[
            pltpu.VMEM((ITERS, 2 * COLS, ROWS), BF16),
            pltpu.VMEM((ITERS, 2 * COLS, ROWS), BF16),
            pltpu.VMEM((ITERS, 2 * COLS, ROWS), BF16),
            pltpu.VMEM((ITERS, ROWS, 128), BF16),
            pltpu.VMEM((ITERS, ROWS, 128), BF16),
            pltpu.VMEM((2 * STRIPE, ROWS), BF16),
            pltpu.VMEM((ITERS, 2, 2 * STRIPE, ROWS), BF16),
            pltpu.VMEM((ITERS, 2, 2 * STRIPE, ROWS), BF16),
            pltpu.VMEM((ITERS, 4, ROWS, ROWS), BF16),
            pltpu.VMEM((3, 2 * COLS, ROWS), BF16),
            pltpu.VMEM((3, 2 * COLS, ROWS), BF16),
            pltpu.VMEM((2 * COLS, ROWS), F32),
            pltpu.VMEM((2 * COLS, ROWS), F32),
            pltpu.VMEM((STRIPE, ROWS), F32),
            pltpu.VMEM((128, 128), F32),
            dma((ITERS, 2)),
            dma((ITERS, 2)),
            dma((ITERS,)),
            dma((ITERS,)),
            dma((ITERS, 2)),
            dma((ITERS, 2)),
            dma((ITERS,)),
            dma((ITERS, N_TP)),
        ],
        compiler_params=pltpu.CompilerParams(
            collective_id=0, has_side_effects=True, vmem_limit_bytes=48 * 2**20
        ),
        cost_estimate=pl.CostEstimate(
            flops=ITERS * 8 * COLS * 1536 * ROWS, bytes_accessed=4 * 2**20, transcendentals=0
        ),
    )(green.reshape(2, COLS, ROWS), hamiltonian, interaction)
    return result.reshape(shape)


def solution(mesh):
    in_specs = (P(None, None, "tp", None, "ta"), P(), P())
    out_specs = P(None, None, "tp", None, "ta")
    return jax.shard_map(shards, mesh=mesh, in_specs=in_specs, out_specs=out_specs, check_vma=False)
```

time: 248 us -> 92.2 us (0.37)
  waiting for transfers between devices: 138 us -> 0 us
  Pallas kernels: 0 us -> 88.7 us
  starting transfers between devices: 54.5 us -> 0 us
  local copies, waits for them, and re-layouts: 25.5 us -> 3.27 us
  between operations: 14.1 us -> 0.01 us
  matrix products: 7.75 us -> 0 us
  other arithmetic: 6.17 us -> 0 us
    pallas_call x0 -> x1, Pallas kernels: none -> 88.7 us  [shards(): pl.pallas_call(kernel, out_shape=jax.ShapeDtypeStruct((2, COLS, ROWS), F3...]
    all_gather x2 -> x0, waiting for transfers between devices: 83.1 us -> none  [shards(): portion = lax.all_gather(sending, 'tp', axis=2, tiled=True)]
    ppermute x8 -> x0, waiting for transfers between devices: 39.5 us -> none  [shifted(): return lax.ppermute(block, axis, route)]
    ppermute x8 -> x0, starting transfers between devices: 37 us -> none  [shifted(): return lax.ppermute(block, axis, route)]
    all_to_all x2 -> x0, starting transfers between devices: 17.4 us -> none  [shards(): lax.all_to_all(nearby, 'tp', split_axis=3, concat_axis=3, tiled=True)]
    all_to_all x2 -> x0, waiting for transfers between devices: 15.8 us -> none  [shards(): lax.all_to_all(nearby, 'tp', split_axis=3, concat_axis=3, tiled=True)]
    dot_general x11 -> x0, matrix products: 7.75 us -> none  [the longest x8 6.35 us: half_dot(): return jnp.dot(left_side, right_side, preferred_element_type=jnp.float32)]
    slice x31 -> x0, local copies, waits for them, and re-layouts: 7.31 us -> none  [the longest x8 4.75 us: shards(): portion[:, position].reshape(2, row_count, block_rows)]
  transfers between devices with their start and end apart: 12 -> 0, of which waited for: 9 -> 0; matrix products, arithmetic and copies ran while one was open for 3% -> 0% of each run, Pallas kernels for 0% -> 0%
where the time goes in v1:
time: 92.2 us; the launch traced here: 92 us
  Pallas kernels  88.7 us (96%)
  local copies, waits for them, and re-layouts  3.27 us (4%)
    pallas_call x1, Pallas kernels, shards(): pl.pallas_call(kernel, out_shape=jax.ShapeDtypeStruct((2, COLS, ROWS), F3...  88.7 us
    unnamed x7, local copies, waits for them, and re-layouts  3.27 us

profile of v1, /device:TPU:1, one launch (start us, length us, event | category | flops | bytes accessed | tf_op | source)
XLA Modules:
  0.0 92.0 jit_solution(14678343049742488576)
XLA Ops:
  0.0 0.0 copy-start
  0.0 1.0 %copy-done = f32[2,8,1,16,512]{4,3,2,1,0:T(8,128)S(1)} copy-done((f32[2,8,1,16,512]{4,3,2,1,0:T(8,128)S(1)}, f32[2,8,1,16,512]{4,3,2,1,0:T(8,128)}, u32[]{:S(2)}) %copy-start) | copy-done | bytes 524312
  1.0 0.0 copy-start.1
  1.0 0.7 copy-done.1
  1.8 0.0 copy-start.2
  1.8 0.7 copy-done.2
  2.5 88.7 %shard_map.37 = f32[2,128,512]{2,1,0:T(8,128)S(1)} custom-call(f32[2,128,512]{2,1,0:T(8,128)S(1)} %bitcast.5, f32[32,32]{1,0:T(8,128)S(1)} %copy-done.1, f32[32,32]{1,0:T(8,128)S(1)} %copy-done.2), custom_call_target="tpu_custom_call" | custom-call | flops 1610612736 | bytes 4194304 | tf_op jit(solution)/shard_map/pallas_call | solution.py:354
  91.2 0.8 copy.6
Async XLA Ops:
  0.0 1.0 %copy-start = (f32[2,8,1,16,512]{4,3,2,1,0:T(8,128)S(1)}, f32[2,8,1,16,512]{4,3,2,1,0:T(8,128)}, u32[]{:S(2)}) copy-start(f32[2,8,1,16,512]{4,3,2,1,0:T(8,128)} %param.3) | copy-start | bytes 1572868
  1.0 0.7 copy-start.1
  1.8 0.7 copy-start.2

commit v2 on v1

--- a/solution.py
+++ b/solution.py
@@ -17,6 +17,7 @@
 ROWS = 512
 COLS = 128
 FACTOR = 1.0 / 32.0
+PIECES = ((0, 2, 0, 256), (0, 1, 0, 64), (2, 1, 64, 64), (5, 1, 128, 128))
 
 MESH = pl.DeviceIdType.MESH
 HIGHEST = lax.Precision.HIGHEST
@@ -35,10 +36,13 @@
 
 
 def kernel(
+    green_hbm,
+    ham_hbm,
+    inter_hbm,
+    out_ref,
     green_ref,
     ham_ref,
     inter_ref,
-    out_ref,
     rounded,
     previous,
     earliest,
@@ -62,6 +66,7 @@
     flip_recv,
     window_send,
     window_recv,
+    input_sem,
 ):
     ta = lax.axis_index("ta")
     tp = lax.axis_index("tp")
@@ -72,8 +77,24 @@
     def ta_plus(k):
         return lax.rem(ta + k + N_TA, N_TA)
 
+    near = zl + 1 - 2 * lax.rem(zl, 2)
+    middle = 2 - zl // 2
+    far = 3 * (1 - zl // 2)
+
+    def stripe_of(q):
+        return pl.ds(pl.multiple_of(q * STRIPE, STRIPE), STRIPE)
+
     def place(dy, z, c):
         return lax.rem(y + dy, N_Y) * 8 + z * 2 + c
+
+    inputs = [
+        pltpu.make_async_copy(src, dst, input_sem.at[n])
+        for n, (src, dst) in enumerate(
+            ((green_hbm, green_ref), (ham_hbm, ham_ref), (inter_hbm, inter_ref))
+        )
+    ]
+    for copy in inputs:
+        copy.start()
 
     barrier = pltpu.get_barrier_semaphore()
 
@@ -113,12 +134,13 @@
         for r in range(2):
             rounded[it, pl.ds(r * COLS, COLS), :] = state[r].astype(BF16)
 
-    def row_copy(it, k):
+    def row_copy(it, n):
+        k, start, count = PIECES[n][1:]
         return remote(
-            rounded.at[it],
-            (previous if k == 1 else earliest).at[it],
-            row_send.at[it, k - 1],
-            row_recv.at[it, k - 1],
+            rounded.at[it, pl.ds(start, count)],
+            (previous if k == 1 else earliest).at[it, pl.ds(start, count)],
+            row_send.at[it, n],
+            row_recv.at[it, n],
             (ta_plus(k), tp),
         )
 
@@ -132,20 +154,21 @@
         )
 
     def send_mirror(it):
-        def send(k, carry):
-            peer = lax.rem(tp + k, N_TP)
-            remote(
-                mirror_out.at[it, pl.ds(pl.multiple_of(peer * STRIPE, STRIPE), STRIPE), :],
-                mirror_in.at[it, pl.ds(pl.multiple_of(tp * STRIPE, STRIPE), STRIPE), :],
-                mirror_send.at[it],
-                mirror_recv.at[it],
-                (ta, peer),
-            ).start()
-            return carry
-
-        lax.fori_loop(1, N_TP, send, 0)
-        own = pl.ds(pl.multiple_of(tp * STRIPE, STRIPE), STRIPE)
-        mirror_in[it, own, :] = mirror_out[it, own, :]
+        for dy in (2, 1, 3, 0):
+            for z in (far, middle, near, zl):
+                for flip_core in (1, 0):
+                    if dy == 0 and z is zl and flip_core == 0:
+                        continue
+                    c = 1 - core if flip_core else core
+                    peer = place(dy, z, c)
+                    remote(
+                        mirror_out.at[it, stripe_of(peer), :],
+                        mirror_in.at[it, stripe_of(tp), :],
+                        mirror_send.at[it],
+                        mirror_recv.at[it],
+                        (ta, peer),
+                    ).start()
+        mirror_in[it, stripe_of(tp), :] = mirror_out[it, stripe_of(tp), :]
 
     def wait_bytes(ref, sem):
         pltpu.make_async_copy(ref, ref, sem).wait()
@@ -183,11 +206,10 @@
         real_square = real * real - imag * imag
         imag_square = 2.0 * real * imag
         coupling = weights[...]
-        own = pl.ds(pl.multiple_of(tp * STRIPE, STRIPE), STRIPE)
-        window[it, 2 * kind, own, :] = (
+        window[it, 2 * kind, y, zl, core] = (
             coupling * (real_square * mirror_real - imag_square * mirror_imag)
         ).astype(BF16)
-        window[it, 2 * kind + 1, own, :] = (
+        window[it, 2 * kind + 1, y, zl, core] = (
             coupling * (real_square * mirror_imag + imag_square * mirror_real)
         ).astype(BF16)
 
@@ -214,26 +236,59 @@
             it, 1, column(state, 0, 1), column(state, 1, 1), mirror_real, mirror_imag
         )
 
-    def block(it, q):
-        return window.at[it, :, pl.ds(pl.multiple_of(q * STRIPE, STRIPE), STRIPE), :]
-
-    def send_block(it, q, target):
+    def send_own(it, kind):
+        part = window.at[it, pl.ds(2 * kind, 2), y, :, core]
+        for z in (near, middle, far):
+            remote(
+                part.at[:, zl],
+                part.at[:, zl],
+                window_send.at[it],
+                window_recv.at[it, kind, zl],
+                (ta, place(0, z, core)),
+            ).start()
+
+    def wait_z(it, kind, z):
+        part = window.at[it, pl.ds(2 * kind, 2), y, :, core]
+        wait_bytes(part.at[:, z], window_recv.at[it, kind, z])
+
+    def pair_part(it, kind, dy, pair):
+        return window.at[
+            it, pl.ds(2 * kind, 2), lax.rem(y + dy, N_Y), pl.ds(2 * pair, 2), core
+        ]
+
+    def send_pair(it, kind, pair):
+        part = pair_part(it, kind, 0, pair)
+        for dy in (2, 1, 3):
+            remote(
+                part,
+                part,
+                window_send.at[it],
+                window_recv.at[it, kind, 4 + 4 * pair + y],
+                (ta, place(dy, zl, core)),
+            ).start()
+
+    def wait_pair(it, kind, dy, pair):
+        wait_bytes(
+            pair_part(it, kind, dy, pair),
+            window_recv.at[it, kind, 4 + 4 * pair + lax.rem(y + dy, N_Y)],
+        )
+
+    def send_sibling(it, kind, dy):
+        j = lax.rem(y + dy, N_Y)
+        part = window.at[it, pl.ds(2 * kind, 2), j, :, core]
         remote(
-            block(it, q), block(it, q), window_send.at[it], window_recv.at[it, q], (ta, target)
+            part,
+            part,
+            window_send.at[it],
+            window_recv.at[it, kind, 12 + j],
+            (ta, place(0, zl, 1 - core)),
         ).start()
 
-    def wait_block(it, q):
-        wait_bytes(block(it, q), window_recv.at[it, q])
-
-    near = zl + 1 - 2 * lax.rem(zl, 2)
-    middle = 2 - zl // 2
-    far = 3 * (1 - zl // 2)
-    z_order = (zl, near, middle, far)
-
-    def send_y(it, q):
-        for dy in (1, 3, 2):
-            send_block(it, q, lax.rem(tp + 8 * dy, N_TP))
-        send_block(it, q, tp + 1 - 2 * core)
+    def wait_sibling(it, kind, dy):
+        j = lax.rem(y + dy, N_Y)
+        wait_bytes(
+            window.at[it, pl.ds(2 * kind, 2), j, :, 1 - core], window_recv.at[it, kind, 12 + j]
+        )
 
     def lefts(it, which, source, keep):
         for r in range(2):
@@ -243,7 +298,10 @@
             straight[which, pl.ds(r * COLS, COLS), :] = half
             crossed[which, pl.ds((1 - r) * COLS, COLS), :] = -half if r == 1 else half
 
-    def multiply(it, dy):
+    def rows_of(it, part, j):
+        return window[it, part, j].reshape(128, ROWS)
+
+    def multiply_combined(it, dy):
         j = lax.rem(y + dy, N_Y)
         lanes = pl.ds(pl.multiple_of(j * 128, 128), 128)
         later = (j * 4 + iota((128, ROWS), 0) // NO) > iota((128, ROWS), 1) // NO
@@ -251,9 +309,9 @@
         new = jnp.where(later, 0.0, 1.0).astype(BF16)
         left_parts, right_parts = [], []
         for r, side in ((0, straight), (1, crossed)):
-            combined = window[it, r, lanes, :]
-            right_parts += [combined * new, combined * old, window[it, 2 + r, lanes, :]]
-            left_parts += [side[which, :, lanes] for which in range(3)]
+            combined = rows_of(it, r, j)
+            right_parts += [combined * new, combined * old]
+            left_parts += [side[which, :, lanes] for which in range(2)]
         product = jnp.dot(
             jnp.concatenate(left_parts, axis=1),
             jnp.concatenate(right_parts, axis=0),
@@ -263,6 +321,14 @@
             total[...] = product
         else:
             total[...] += product
+
+    def multiply_middle(it):
+        total[...] += sum(
+            jnp.dot(
+                side[2], window[it, 2 + r].reshape(ROWS, ROWS), preferred_element_type=F32
+            )
+            for r, side in ((0, straight), (1, crossed))
+        )
 
     def hamilton_term(state):
         for r in range(2):
@@ -284,6 +350,8 @@
         same = iota((128, 128), 0) // NO == iota((128, 128), 1) // NO
         blocked[...] = jnp.where(same, across, 0.0)
 
+    for copy in inputs:
+        copy.wait()
     build_mirror(green_ref, 0)
     build_rounded(green_ref, 0)
     pl.semaphore_wait(barrier, N_TP - 1 + 2)
@@ -293,46 +361,66 @@
         if it:
             build_mirror(state, it)
             build_rounded(state, it)
+        rows = [row_copy(it, n) for n in range(len(PIECES))]
+
+        def start_rows(stage):
+            for piece, copy in zip(PIECES, rows):
+                if piece[0] == stage:
+                    copy.start()
+
+        def wait_rows(k):
+            for piece, copy in zip(PIECES, rows):
+                if piece[1] == k:
+                    copy.wait_recv()
+
         send_mirror(it)
-        rows = [row_copy(it, 2), row_copy(it, 1)]
-        for copy in rows:
-            copy.start()
+        start_rows(0)
         if it == 0:
             prepare()
         lefts(it, 0, rounded, None)
         wait_bytes(mirror_in.at[it, pl.ds(0, 31 * STRIPE), :], mirror_recv.at[it])
+        start_rows(1)
         flip(it)
         flips = [flip_copy(it, 1), flip_copy(it, 2)]
         for copy in flips:
             copy.start()
+        start_rows(2)
         hamilton_term(state)
         flips[1].wait_recv()
         sigma_combined(state, it)
+        send_own(it, 0)
+        start_rows(3)
         flips[0].wait_recv()
         sigma_middle(state, it)
-        for z in (near, middle, far):
-            send_block(it, tp, place(0, z, core))
-        send_y(it, tp)
-        for z in (near, middle, far):
-            q = place(0, z, core)
-            wait_block(it, q)
-            send_y(it, q)
-        rows[0].wait_recv()
-        lefts(it, 2 - 1, earliest, ta >= 2)
-        rows[1].wait_recv()
+        send_own(it, 1)
+        start_rows(4)
+        own_pair = zl // 2
+        wait_rows(2)
+        lefts(it, 1, earliest, ta >= 2)
+        for kind in range(2):
+            wait_z(it, kind, near)
+            send_pair(it, kind, own_pair)
+        for kind in range(2):
+            wait_z(it, kind, middle)
+            wait_z(it, kind, far)
+            send_pair(it, kind, 1 - own_pair)
+            send_sibling(it, kind, 0)
+        start_rows(5)
+        wait_sibling(it, 0, 0)
+        multiply_combined(it, 0)
+        for kind in range(2):
+            for dy in (1, 3, 2):
+                wait_pair(it, kind, dy, own_pair)
+                wait_pair(it, kind, dy, 1 - own_pair)
+                send_sibling(it, kind, dy)
+        for dy in (1, 3, 2):
+            wait_sibling(it, 0, dy)
+            multiply_combined(it, dy)
+        wait_rows(1)
         lefts(it, 2, previous, ta >= 1)
-        for z in z_order:
-            wait_block(it, place(0, z, 1 - core))
-        multiply(it, 0)
-        for z in z_order:
-            for dy in (1, 3, 2):
-                q = place(dy, z, core)
-                wait_block(it, q)
-                send_block(it, q, tp + 1 - 2 * core)
-        for dy in (1, 3, 2):
-            for z in z_order:
-                wait_block(it, place(dy, z, 1 - core))
-            multiply(it, dy)
+        for dy in range(4):
+            wait_sibling(it, 1, dy)
+        multiply_middle(it)
         out_real = state[0] + 0.5 * (
             hamilton[pl.ds(COLS, COLS), :] + FACTOR * total[pl.ds(COLS, COLS), :]
         )
@@ -344,7 +432,9 @@
         wait_bytes(mirror_out.at[it, pl.ds(0, 31 * STRIPE), :], mirror_send.at[it])
         for copy in rows + flips:
             copy.wait_send()
-        wait_bytes(window.at[it, :, pl.ds(0, 31 * STRIPE), :], window_send.at[it])
+        wait_bytes(window.at[it, :, pl.ds(0, 3)], window_send.at[it])
+        wait_bytes(window.at[it, :, 3, pl.ds(0, 3)], window_send.at[it])
+        wait_bytes(window.at[it, :, 3, 3, 0], window_send.at[it])
 
 
 def shards(green, hamiltonian, interaction):
@@ -354,9 +444,12 @@
     result = pl.pallas_call(
         kernel,
         out_shape=jax.ShapeDtypeStruct((2, COLS, ROWS), F32),
-        in_specs=[whole] * 3,
+        in_specs=[pl.BlockSpec(memory_space=pltpu.HBM)] * 3,
         out_specs=whole,
         scratch_shapes=[
+            pltpu.VMEM((2, COLS, ROWS), F32),
+            pltpu.VMEM((NO, NO), F32),
+            pltpu.VMEM((NO, NO), F32),
             pltpu.VMEM((ITERS, 2 * COLS, ROWS), BF16),
             pltpu.VMEM((ITERS, 2 * COLS, ROWS), BF16),
             pltpu.VMEM((ITERS, 2 * COLS, ROWS), BF16),
@@ -365,21 +458,22 @@
             pltpu.VMEM((2 * STRIPE, ROWS), BF16),
             pltpu.VMEM((ITERS, 2, 2 * STRIPE, ROWS), BF16),
             pltpu.VMEM((ITERS, 2, 2 * STRIPE, ROWS), BF16),
-            pltpu.VMEM((ITERS, 4, ROWS, ROWS), BF16),
+            pltpu.VMEM((ITERS, 4, N_Y, N_Z, 2, STRIPE, ROWS), BF16),
             pltpu.VMEM((3, 2 * COLS, ROWS), BF16),
             pltpu.VMEM((3, 2 * COLS, ROWS), BF16),
             pltpu.VMEM((2 * COLS, ROWS), F32),
             pltpu.VMEM((2 * COLS, ROWS), F32),
             pltpu.VMEM((STRIPE, ROWS), F32),
             pltpu.VMEM((128, 128), F32),
-            dma((ITERS, 2)),
-            dma((ITERS, 2)),
+            dma((ITERS, len(PIECES))),
+            dma((ITERS, len(PIECES))),
             dma((ITERS,)),
             dma((ITERS,)),
             dma((ITERS, 2)),
             dma((ITERS, 2)),
             dma((ITERS,)),
-            dma((ITERS, N_TP)),
+            dma((ITERS, 2, 16)),
+            dma((3,)),
         ],
         compiler_params=pltpu.CompilerParams(
             collective_id=0, has_side_effects=True, vmem_limit_bytes=48 * 2**20

time: 92.2 us -> 76 us (0.82)
  Pallas kernels: 88.7 us -> 72.5 us
    pallas_call x1, Pallas kernels: 88.7 us -> 72.5 us  [shards(): pl.pallas_call(kernel, out_shape=jax.ShapeDtypeStruct((2, COLS, ROWS), F3...]
where the time goes in v2:
time: 76 us; the launch traced here: 75.8 us
  Pallas kernels  72.5 us (95%)
  local copies, waits for them, and re-layouts  3.27 us (4%)
    pallas_call x1, Pallas kernels, shards(): pl.pallas_call(kernel, out_shape=jax.ShapeDtypeStruct((2, COLS, ROWS), F3...  72.5 us
    unnamed x7, local copies, waits for them, and re-layouts  3.27 us

profile of v2, /device:TPU:1, one launch (start us, length us, event | category | flops | bytes accessed | tf_op | source)
XLA Modules:
  0.0 75.8 jit_solution(12471089174302719606)
XLA Ops:
  0.0 0.0 copy-start
  0.0 1.0 %copy-done = f32[2,8,1,16,512]{4,3,2,1,0:T(8,128)S(1)} copy-done((f32[2,8,1,16,512]{4,3,2,1,0:T(8,128)S(1)}, f32[2,8,1,16,512]{4,3,2,1,0:T(8,128)}, u32[]{:S(2)}) %copy-start) | copy-done | bytes 524312
  1.0 0.0 copy-start.1
  1.0 0.7 copy-done.1
  1.8 0.0 copy-start.2
  1.8 0.7 copy-done.2
  2.5 72.5 %shard_map.37 = f32[2,128,512]{2,1,0:T(8,128)S(1)} custom-call(f32[2,128,512]{2,1,0:T(8,128)S(1)} %bitcast.5, f32[32,32]{1,0:T(8,128)S(1)} %copy-done.1, f32[32,32]{1,0:T(8,128)S(1)} %copy-done.2), custom_call_target="tpu_custom_call" | custom-call | flops 1610612736 | bytes 4194304 | tf_op jit(solution)/shard_map/pallas_call | solution.py:444
  75.0 0.8 %copy.6 = f32[2,8,1,16,512]{4,3,2,1,0:T(8,128)} copy(f32[2,8,1,16,512]{4,3,2,1,0:T(8,128)S(1)} %bitcast.4) | data formatting | bytes 1048576
Async XLA Ops:
  0.0 1.0 %copy-start = (f32[2,8,1,16,512]{4,3,2,1,0:T(8,128)S(1)}, f32[2,8,1,16,512]{4,3,2,1,0:T(8,128)}, u32[]{:S(2)}) copy-start(f32[2,8,1,16,512]{4,3,2,1,0:T(8,128)} %param.3) | copy-start | bytes 1572868
  1.0 0.7 copy-start.1
  1.8 0.7 copy-start.2

commit v3 on v2

v3 whole, which is shorter than its diff:
```python
import functools

import jax
import jax.numpy as jnp
from jax import lax
from jax.experimental import pallas as pl
from jax.experimental.pallas import tpu as pltpu
from jax.sharding import PartitionSpec as P

NO = 32
ITERS = 2
N_TA = 8
N_TP = 32
N_Y = 4
N_Z = 4
STRIPE = 16
ROWS = 512
COLS = 128
FACTOR = 1.0 / 32.0
PIECES = ((4, 2, 0, 256), (0, 1, 0, 128), (5, 1, 128, 128))

MESH = pl.DeviceIdType.MESH
HIGHEST = lax.Precision.HIGHEST
F32 = jnp.float32
BF16 = jnp.bfloat16


def iota(shape, dim):
    return lax.broadcasted_iota(jnp.int32, shape, dim)


def exact_dot(left, right, contract=((1,), (0,))):
    return lax.dot_general(
        left, right, (contract, ((), ())), precision=HIGHEST, preferred_element_type=F32
    )


def kernel(
    green_hbm,
    ham_hbm,
    inter_hbm,
    out_ref,
    green_ref,
    ham_ref,
    inter_ref,
    rounded,
    previous,
    earliest,
    stage_out,
    stage_in,
    mirror_out,
    mirror_in,
    flipped,
    window,
    straight,
    crossed,
    total,
    hamilton,
    weights,
    blocked,
    row_send,
    row_recv,
    stage_send,
    stage_recv,
    mirror_send,
    mirror_recv,
    window_send,
    window_recv,
    input_sem,
):
    ta = lax.axis_index("ta")
    tp = lax.axis_index("tp")
    y = tp // 8
    zl = lax.rem(tp // 2, 4)
    core = lax.rem(tp, 2)

    def ta_plus(k):
        return lax.rem(ta + k + N_TA, N_TA)

    near = zl + 1 - 2 * lax.rem(zl, 2)
    middle = 2 - zl // 2
    far = 3 * (1 - zl // 2)
    z_order = (zl, near, middle, far)

    def stripe_of(q):
        return pl.ds(pl.multiple_of(q * STRIPE, STRIPE), STRIPE)

    def place(dy, z, c):
        return lax.rem(y + dy, N_Y) * 8 + z * 2 + c

    inputs = [
        pltpu.make_async_copy(src, dst, input_sem.at[n])
        for n, (src, dst) in enumerate(
            ((green_hbm, green_ref), (ham_hbm, ham_ref), (inter_hbm, inter_ref))
        )
    ]
    for copy in inputs:
        copy.start()

    barrier = pltpu.get_barrier_semaphore()

    for dy in (1, 2, 3):
        pl.semaphore_signal(
            barrier, inc=1, device_id=(ta, place(dy, zl, core)), device_id_type=MESH
        )
    for k in (1, 2, 0):
        for z in (far, middle, near, zl):
            for other in (1, 0):
                if k == 0 and z is zl and other == 0:
                    continue
                c = 1 - core if other else core
                pl.semaphore_signal(
                    barrier,
                    inc=1,
                    device_id=(ta_plus(-k), place(0, z, c)),
                    device_id_type=MESH,
                )

    def remote(src, dst, send, recv, target):
        return pltpu.make_async_remote_copy(
            src_ref=src,
            dst_ref=dst,
            send_sem=send,
            recv_sem=recv,
            device_id=target,
            device_id_type=MESH,
        )

    def build_stage(state, it):
        for k in range(3):
            group = pl.multiple_of(ta_plus(k) * STRIPE, STRIPE)
            for r in range(2):
                piece = state[r, pl.ds(group, STRIPE), :].astype(BF16)
                for j in range(N_Y):
                    stage_out[it, j, pl.ds((2 * k + r) * STRIPE, STRIPE), :] = piece[
                        :, j * 128 : (j + 1) * 128
                    ]

    def build_rounded(state, it):
        for r in range(2):
            rounded[it, pl.ds(r * COLS, COLS), :] = state[r].astype(BF16)

    def row_copy(it, n):
        k, start, count = PIECES[n][1:]
        return remote(
            rounded.at[it, pl.ds(start, count)],
            (previous if k == 1 else earliest).at[it, pl.ds(start, count)],
            row_send.at[it, n],
            row_recv.at[it, n],
            (ta_plus(k), tp),
        )

    def stage_copy(it, dy):
        j = lax.rem(y + dy, N_Y)
        return remote(
            stage_out.at[it, j],
            stage_in.at[it, y],
            stage_send.at[it, dy - 1],
            stage_recv.at[it, dy - 1],
            (ta, place(dy, zl, core)),
        )

    def build_mirror(it):
        stage_in[it, y] = stage_out[it, y]
        for k in (1, 2, 0):
            stacked = jnp.concatenate(
                [stage_in[it, j, pl.ds(2 * k * STRIPE, 2 * STRIPE), :] for j in range(N_Y)],
                axis=0,
            )
            mirror_out[it, k] = stacked.astype(F32).T.astype(BF16)
            send_mirror(it, k)
        own = stripe_of(zl * 2 + core)
        mirror_in[it, 0, own, :] = mirror_out[it, 0, own, :]

    def send_mirror(it, k):
        for z in (far, middle, near, zl):
            for other in (1, 0):
                if k == 0 and z is zl and other == 0:
                    continue
                c = 1 - core if other else core
                remote(
                    mirror_out.at[it, k, stripe_of(z * 2 + c), :],
                    mirror_in.at[it, k, stripe_of(zl * 2 + core), :],
                    mirror_send.at[it, k],
                    mirror_recv.at[it, k],
                    (ta_plus(k), place(0, z, c)),
                ).start()

    def mirror_bytes(ref, it, k):
        return ref.at[it, k] if k else ref.at[it, 0, pl.ds(0, 7 * STRIPE), :]

    def wait_bytes(ref, sem):
        pltpu.make_async_copy(ref, ref, sem).wait()

    def flip(it, k):
        piece = iota((STRIPE, 128), 1) // STRIPE
        parts = [
            mirror_in[it, k, pl.ds(i * STRIPE, STRIPE), :].astype(F32) for i in range(8)
        ]
        for bit in (1, 2, 4):
            low = (piece // bit) % 2 == 0
            for i in range(8):
                if i & bit:
                    continue
                first, second = parts[i], parts[i | bit]
                parts[i] = jnp.where(low, first, pltpu.roll(second, STRIPE * bit, 1))
                parts[i | bit] = jnp.where(
                    low, pltpu.roll(first, 128 - STRIPE * bit, 1), second
                )
        for j in range(N_Y):
            for r in range(2):
                flipped[k, r, :, pl.ds(j * 128, 128)] = parts[2 * j + r]

    def column(state, r, k):
        group = pl.multiple_of(ta_plus(-k) * STRIPE, STRIPE)
        return state[r, pl.ds(group, STRIPE), :]

    def self_energy(it, kind, real, imag, mirror_real, mirror_imag):
        real_square = real * real - imag * imag
        imag_square = 2.0 * real * imag
        coupling = weights[...]
        window[it, 2 * kind, y, zl, core] = (
            coupling * (real_square * mirror_real - imag_square * mirror_imag)
        ).astype(BF16)
        window[it, 2 * kind + 1, y, zl, core] = (
            coupling * (real_square * mirror_imag + imag_square * mirror_real)
        ).astype(BF16)

    def sigma_combined(state, it):
        later = iota((STRIPE, ROWS), 1) // NO < tp // 2
        real, imag = (
            jnp.where(later, column(state, r, 2), column(state, r, 0)) for r in range(2)
        )
        mirror_real, mirror_imag = (
            jnp.where(later, flipped[2, r], flipped[0, r]) for r in range(2)
        )
        self_energy(it, 0, real, imag, mirror_real, mirror_imag)

    def sigma_middle(state, it):
        self_energy(
            it, 1, column(state, 0, 1), column(state, 1, 1), flipped[1, 0], flipped[1, 1]
        )

    def send_own(it, kind):
        part = window.at[it, pl.ds(2 * kind, 2), y, :, core]
        for z in (near, middle, far):
            remote(
                part.at[:, zl],
                part.at[:, zl],
                window_send.at[it],
                window_recv.at[it, kind, zl],
                (ta, place(0, z, core)),
            ).start()

    def wait_z(it, kind, z):
        part = window.at[it, pl.ds(2 * kind, 2), y, :, core]
        wait_bytes(part.at[:, z], window_recv.at[it, kind, z])

    def y_part(it, kind, dy, piece):
        part = window.at[it, pl.ds(2 * kind, 2), lax.rem(y + dy, N_Y)]
        return part.at[:, z_order[piece], core]

    def y_copy(it, kind, piece, source, target):
        part = y_part(it, kind, source, piece)
        return remote(
            part,
            part,
            window_send.at[it],
            window_recv.at[it, kind, 4 + 4 * piece + lax.rem(y + source, N_Y)],
            (ta, place(target, zl, core)),
        )

    def send_y(it, kind, piece):
        for dy in (2, 1, 3) if piece == 3 else (1, 3):
            y_copy(it, kind, piece, 0, dy).start()

    def wait_y(it, kind, piece, dy):
        wait_bytes(
            y_part(it, kind, dy, piece),
            window_recv.at[it, kind, 4 + 4 * piece + lax.rem(y + dy, N_Y)],
        )

    def relay(it, kind, piece):
        source, target = ((3, 1), (1, 3))[kind]
        wait_y(it, kind, piece, source)
        y_copy(it, kind, piece, source, target).start()

    def send_sibling(it, kind, dy):
        j = lax.rem(y + dy, N_Y)
        part = window.at[it, pl.ds(2 * kind, 2), j, :, core]
        remote(
            part,
            part,
            window_send.at[it],
            window_recv.at[it, kind, 20 + j],
            (ta, place(0, zl, 1 - core)),
        ).start()

    def wait_sibling(it, kind, dy):
        j = lax.rem(y + dy, N_Y)
        wait_bytes(
            window.at[it, pl.ds(2 * kind, 2), j, :, 1 - core], window_recv.at[it, kind, 20 + j]
        )

    def lefts(it, which, source, keep):
        for r in range(2):
            half = source[it, pl.ds(r * COLS, COLS), :]
            if keep is not None:
                half = jnp.where(keep, half, jnp.zeros_like(half))
            straight[which, pl.ds(r * COLS, COLS), :] = half
            crossed[which, pl.ds((1 - r) * COLS, COLS), :] = -half if r == 1 else half

    def rows_of(it, part, j):
        return window[it, part, j].reshape(128, ROWS)

    def multiply_combined(it, dy):
        j = lax.rem(y + dy, N_Y)
        lanes = pl.ds(pl.multiple_of(j * 128, 128), 128)
        later = (j * 4 + iota((128, ROWS), 0) // NO) > iota((128, ROWS), 1) // NO
        old = jnp.where(later, 1.0, 0.0).astype(BF16)
        new = jnp.where(later, 0.0, 1.0).astype(BF16)
        left_parts, right_parts = [], []
        for r, side in ((0, straight), (1, crossed)):
            combined = rows_of(it, r, j)
            right_parts += [combined * new, combined * old]
            left_parts += [side[which, :, lanes] for which in range(2)]
        product = jnp.dot(
            jnp.concatenate(left_parts, axis=1),
            jnp.concatenate(right_parts, axis=0),
            preferred_element_type=F32,
        )
        if dy == 0:
            total[...] = product
        else:
            total[...] += product

    def multiply_middle(it, dy):
        j = lax.rem(y + dy, N_Y)
        lanes = pl.ds(pl.multiple_of(j * 128, 128), 128)
        total[...] += jnp.dot(
            jnp.concatenate([straight[2, :, lanes], crossed[2, :, lanes]], axis=1),
            jnp.concatenate([rows_of(it, 2, j), rows_of(it, 3, j)], axis=0),
            preferred_element_type=F32,
        )

    def hamilton_term(state):
        for r in range(2):
            for b in range(4):
                lanes = pl.ds(b * 128, 128)
                hamilton[pl.ds(r * COLS, COLS), lanes] = exact_dot(
                    state[r, :, lanes], blocked[...]
                )

    def prepare():
        squared = inter_ref[...] * inter_ref[...]
        pick = (iota((STRIPE, NO), 1) == core * STRIPE + iota((STRIPE, NO), 0)).astype(F32)
        picked = exact_dot(pick, squared, ((1,), (1,)))
        spread = (lax.rem(iota((NO, ROWS), 1), NO) == iota((NO, ROWS), 0)).astype(F32)
        weights[...] = exact_dot(picked, spread)
        tall = (lax.rem(iota((128, NO), 0), NO) == iota((128, NO), 1)).astype(F32)
        wide = (lax.rem(iota((NO, 128), 1), NO) == iota((NO, 128), 0)).astype(F32)
        across = exact_dot(exact_dot(tall, ham_ref[...], ((1,), (1,))), wide)
        same = iota((128, 128), 0) // NO == iota((128, 128), 1) // NO
        blocked[...] = jnp.where(same, across, 0.0)

    for copy in inputs:
        copy.wait()
    build_stage(green_ref, 0)
    pl.semaphore_wait(barrier, 26)

    for it in range(ITERS):
        state = green_ref if it == 0 else out_ref
        if it:
            build_stage(state, it)
        stages = [stage_copy(it, dy) for dy in (1, 2, 3)]
        for n in (1, 0, 2):
            stages[n].start()
        build_rounded(state, it)
        rows = [row_copy(it, n) for n in range(len(PIECES))]

        def start_rows(stage):
            for piece, copy in zip(PIECES, rows):
                if piece[0] == stage:
                    copy.start()

        def wait_rows(k):
            for piece, copy in zip(PIECES, rows):
                if piece[1] == k:
                    copy.wait_recv()

        start_rows(0)
        if it == 0:
            prepare()
        lefts(it, 0, rounded, None)
        for copy in stages:
            copy.wait_recv()
        build_mirror(it)
        start_rows(1)
        hamilton_term(state)
        for k in (0, 2):
            wait_bytes(mirror_bytes(mirror_in, it, k), mirror_recv.at[it, k])
            flip(it, k)
        sigma_combined(state, it)
        send_own(it, 0)
        send_y(it, 0, 0)
        start_rows(3)
        wait_bytes(mirror_bytes(mirror_in, it, 1), mirror_recv.at[it, 1])
        flip(it, 1)
        sigma_middle(state, it)
        send_own(it, 1)
        send_y(it, 1, 0)
        start_rows(4)
        for kind in range(2):
            wait_z(it, kind, near)
            send_y(it, kind, 1)
        for kind in range(2):
            relay(it, kind, 0)
        for kind in range(2):
            wait_z(it, kind, middle)
            send_y(it, kind, 2)
        for kind in range(2):
            relay(it, kind, 1)
        for kind in range(2):
            wait_z(it, kind, far)
            send_y(it, kind, 3)
            send_sibling(it, kind, 0)
        start_rows(5)
        for kind in range(2):
            relay(it, kind, 2)
        for kind in range(2):
            dy = 3 if kind == 0 else 1
            wait_y(it, kind, 3, dy)
            send_sibling(it, kind, dy)
        for kind in range(2):
            dy = 1 if kind == 0 else 3
            for piece in range(4):
                wait_y(it, kind, piece, dy)
            send_sibling(it, kind, dy)
        wait_rows(2)
        lefts(it, 1, earliest, ta >= 2)
        wait_sibling(it, 0, 0)
        multiply_combined(it, 0)
        for piece in range(4):
            wait_y(it, 0, piece, 2)
        send_sibling(it, 0, 2)
        for dy in (3, 1):
            wait_sibling(it, 0, dy)
            multiply_combined(it, dy)
        for piece in range(4):
            wait_y(it, 1, piece, 2)
        send_sibling(it, 1, 2)
        wait_rows(1)
        lefts(it, 2, previous, ta >= 1)
        for dy in (0, 1, 3):
            wait_sibling(it, 1, dy)
            multiply_middle(it, dy)
        wait_sibling(it, 0, 2)
        multiply_combined(it, 2)
        wait_sibling(it, 1, 2)
        multiply_middle(it, 2)
        out_real = state[0] + 0.5 * (
            hamilton[pl.ds(COLS, COLS), :] + FACTOR * total[pl.ds(COLS, COLS), :]
        )
        out_imag = state[1] - 0.5 * (
            hamilton[pl.ds(0, COLS), :] + FACTOR * total[pl.ds(0, COLS), :]
        )
        out_ref[0] = out_real
        out_ref[1] = out_imag
        for k in range(3):
            wait_bytes(mirror_bytes(mirror_out, it, k), mirror_send.at[it, k])
        for copy in rows + stages:
            copy.wait_send()
        wait_bytes(window.at[it, :, pl.ds(0, 3)], window_send.at[it])
        wait_bytes(window.at[it, :, 3, pl.ds(0, 3)], window_send.at[it])
        wait_bytes(window.at[it, :, 3, 3, 0], window_send.at[it])


def shards(green, hamiltonian, interaction):
    shape = green.shape
    whole = pl.BlockSpec(memory_space=pltpu.VMEM)
    dma = pltpu.SemaphoreType.DMA
    result = pl.pallas_call(
        kernel,
        out_shape=jax.ShapeDtypeStruct((2, COLS, ROWS), F32),
        in_specs=[pl.BlockSpec(memory_space=pltpu.HBM)] * 3,
        out_specs=whole,
        scratch_shapes=[
            pltpu.VMEM((2, COLS, ROWS), F32),
            pltpu.VMEM((NO, NO), F32),
            pltpu.VMEM((NO, NO), F32),
            pltpu.VMEM((ITERS, 2 * COLS, ROWS), BF16),
            pltpu.VMEM((ITERS, 2 * COLS, ROWS), BF16),
            pltpu.VMEM((ITERS, 2 * COLS, ROWS), BF16),
            pltpu.VMEM((ITERS, N_Y, 6 * STRIPE, 128), BF16),
            pltpu.VMEM((ITERS, N_Y, 6 * STRIPE, 128), BF16),
            pltpu.VMEM((ITERS, 3, 128, 128), BF16),
            pltpu.VMEM((ITERS, 3, 128, 128), BF16),
            pltpu.VMEM((3, 2, STRIPE, ROWS), F32),
            pltpu.VMEM((ITERS, 4, N_Y, N_Z, 2, STRIPE, ROWS), BF16),
            pltpu.VMEM((3, 2 * COLS, ROWS), BF16),
            pltpu.VMEM((3, 2 * COLS, ROWS), BF16),
            pltpu.VMEM((2 * COLS, ROWS), F32),
            pltpu.VMEM((2 * COLS, ROWS), F32),
            pltpu.VMEM((STRIPE, ROWS), F32),
            pltpu.VMEM((128, 128), F32),
            dma((ITERS, len(PIECES))),
            dma((ITERS, len(PIECES))),
            dma((ITERS, 3)),
            dma((ITERS, 3)),
            dma((ITERS, 3)),
            dma((ITERS, 3)),
            dma((ITERS,)),
            dma((ITERS, 2, 24)),
            dma((3,)),
        ],
        compiler_params=pltpu.CompilerParams(
            collective_id=0, has_side_effects=True, vmem_limit_bytes=63 * 2**20 + 900000
        ),
        cost_estimate=pl.CostEstimate(
            flops=ITERS * 8 * COLS * 1536 * ROWS, bytes_accessed=4 * 2**20, transcendentals=0
        ),
    )(green.reshape(2, COLS, ROWS), hamiltonian, interaction)
    return result.reshape(shape)


def solution(mesh):
    in_specs = (P(None, None, "tp", None, "ta"), P(), P())
    out_specs = P(None, None, "tp", None, "ta")
    return jax.shard_map(shards, mesh=mesh, in_specs=in_specs, out_specs=out_specs, check_vma=False)
```

time: 76 us -> 70.3 us (0.925)
  Pallas kernels: 72.5 us -> 68.2 us
  local copies, waits for them, and re-layouts: 3.27 us -> 1.88 us
    pallas_call x1, Pallas kernels: 72.5 us -> 68.2 us  [shards(): pl.pallas_call(kernel, out_shape=jax.ShapeDtypeStruct((2, COLS, ROWS), F3...]
    unnamed x7 -> x1, local copies, waits for them, and re-layouts: 3.27 us -> 1.88 us
where the time goes in v3:
time: 70.3 us; the launch traced here: 70.1 us
  Pallas kernels  68.2 us (97%)
  local copies, waits for them, and re-layouts  1.88 us (3%)
    pallas_call x1, Pallas kernels, shards(): pl.pallas_call(kernel, out_shape=jax.ShapeDtypeStruct((2, COLS, ROWS), F3...  68.2 us
    unnamed x1, local copies, waits for them, and re-layouts  1.88 us

profile of v3, /device:TPU:1, one launch (start us, length us, event | category | flops | bytes accessed | tf_op | source)
XLA Modules:
  0.0 70.1 jit_solution(3204182470363626596)
XLA Ops:
  0.0 68.2 %shard_map.37 = f32[2,128,512]{2,1,0:T(8,128)} custom-call(f32[2,128,512]{2,1,0:T(8,128)} %bitcast.5, f32[32,32]{1,0:T(8,128)} %ham_hbm.1, f32[32,32]{1,0:T(8,128)} %inter_hbm.1), custom_call_target="tpu_custom_call" | custom-call | flops 1610612736 | bytes 4194304 | tf_op jit(solution)/shard_map/pallas_call | solution.py:482
  68.2 1.9 %copy.6 = f32[2,8,1,16,512]{4,3,2,1,0:T(8,128)} copy(f32[2,8,1,16,512]{4,3,2,1,0:T(8,128)} %bitcast.4) | data formatting | bytes 1048576

commit v4 on v3

--- a/solution.py
+++ b/solution.py
@@ -17,7 +17,7 @@
 ROWS = 512
 COLS = 128
 FACTOR = 1.0 / 32.0
-PIECES = ((4, 2, 0, 256), (0, 1, 0, 128), (5, 1, 128, 128))
+PIECES = ((1, 2, 0, 256), (0, 1, 0, 128), (5, 1, 128, 128))
 
 MESH = pl.DeviceIdType.MESH
 HIGHEST = lax.Precision.HIGHEST
@@ -302,6 +302,29 @@
             window.at[it, pl.ds(2 * kind, 2), j, :, 1 - core], window_recv.at[it, kind, 20 + j]
         )
 
+    def last_part(it, kind, pair, c):
+        j = lax.rem(y + 2, N_Y)
+        return window.at[it, pl.ds(2 * kind, 2), j, pl.ds(2 * pair, 2), c]
+
+    def pass_last(it, kind):
+        for half in range(2):
+            pair = zl // 2 if half == 0 else 1 - zl // 2
+            for piece in (2 * half, 2 * half + 1):
+                wait_y(it, kind, piece, 2)
+            part = last_part(it, kind, pair, core)
+            remote(
+                part,
+                part,
+                window_send.at[it],
+                window_recv.at[it, kind, 24 + half],
+                (ta, place(0, zl, 1 - core)),
+            ).start()
+
+    def wait_last(it, kind):
+        for half in range(2):
+            pair = zl // 2 if half == 0 else 1 - zl // 2
+            wait_bytes(last_part(it, kind, pair, 1 - core), window_recv.at[it, kind, 24 + half])
+
     def lefts(it, which, source, keep):
         for r in range(2):
             half = source[it, pl.ds(r * COLS, COLS), :]
@@ -334,14 +357,22 @@
         else:
             total[...] += product
 
-    def multiply_middle(it, dy):
-        j = lax.rem(y + dy, N_Y)
-        lanes = pl.ds(pl.multiple_of(j * 128, 128), 128)
-        total[...] += jnp.dot(
-            jnp.concatenate([straight[2, :, lanes], crossed[2, :, lanes]], axis=1),
-            jnp.concatenate([rows_of(it, 2, j), rows_of(it, 3, j)], axis=0),
-            preferred_element_type=F32,
-        )
+    def multiply_middle(it, r):
+        left = previous[it, pl.ds(r * COLS, COLS), :]
+        left = jnp.where(ta >= 1, left, jnp.zeros_like(left))
+        with_real, with_imag = (
+            jnp.dot(
+                left, window[it, 2 + part].reshape(ROWS, ROWS), preferred_element_type=F32
+            )
+            for part in range(2)
+        )
+        top, bottom = pl.ds(0, COLS), pl.ds(COLS, COLS)
+        if r == 0:
+            total[top, :] += with_real
+            total[bottom, :] += with_imag
+        else:
+            total[top, :] -= with_imag
+            total[bottom, :] += with_real
 
     def hamilton_term(state):
         for r in range(2):
@@ -368,6 +399,7 @@
     build_stage(green_ref, 0)
     pl.semaphore_wait(barrier, 26)
 
+    started = []
     for it in range(ITERS):
         state = green_ref if it == 0 else out_ref
         if it:
@@ -440,24 +472,19 @@
         lefts(it, 1, earliest, ta >= 2)
         wait_sibling(it, 0, 0)
         multiply_combined(it, 0)
-        for piece in range(4):
-            wait_y(it, 0, piece, 2)
-        send_sibling(it, 0, 2)
+        pass_last(it, 0)
         for dy in (3, 1):
             wait_sibling(it, 0, dy)
             multiply_combined(it, dy)
-        for piece in range(4):
-            wait_y(it, 1, piece, 2)
-        send_sibling(it, 1, 2)
-        wait_rows(1)
-        lefts(it, 2, previous, ta >= 1)
+        pass_last(it, 1)
+        wait_last(it, 0)
+        multiply_combined(it, 2)
         for dy in (0, 1, 3):
             wait_sibling(it, 1, dy)
-            multiply_middle(it, dy)
-        wait_sibling(it, 0, 2)
-        multiply_combined(it, 2)
-        wait_sibling(it, 1, 2)
-        multiply_middle(it, 2)
+        wait_last(it, 1)
+        for r in range(2):
+            rows[1 + r].wait_recv()
+            multiply_middle(it, r)
         out_real = state[0] + 0.5 * (
             hamilton[pl.ds(COLS, COLS), :] + FACTOR * total[pl.ds(COLS, COLS), :]
         )
@@ -466,9 +493,12 @@
         )
         out_ref[0] = out_real
         out_ref[1] = out_imag
+        started.append(rows + stages)
+
+    for it in range(ITERS):
         for k in range(3):
             wait_bytes(mirror_bytes(mirror_out, it, k), mirror_send.at[it, k])
-        for copy in rows + stages:
+        for copy in started[it]:
             copy.wait_send()
         wait_bytes(window.at[it, :, pl.ds(0, 3)], window_send.at[it])
         wait_bytes(window.at[it, :, 3, pl.ds(0, 3)], window_send.at[it])
@@ -497,8 +527,8 @@
             pltpu.VMEM((ITERS, 3, 128, 128), BF16),
             pltpu.VMEM((3, 2, STRIPE, ROWS), F32),
             pltpu.VMEM((ITERS, 4, N_Y, N_Z, 2, STRIPE, ROWS), BF16),
-            pltpu.VMEM((3, 2 * COLS, ROWS), BF16),
-            pltpu.VMEM((3, 2 * COLS, ROWS), BF16),
+            pltpu.VMEM((2, 2 * COLS, ROWS), BF16),
+            pltpu.VMEM((2, 2 * COLS, ROWS), BF16),
             pltpu.VMEM((2 * COLS, ROWS), F32),
             pltpu.VMEM((2 * COLS, ROWS), F32),
             pltpu.VMEM((STRIPE, ROWS), F32),
@@ -510,7 +540,7 @@
             dma((ITERS, 3)),
             dma((ITERS, 3)),
             dma((ITERS,)),
-            dma((ITERS, 2, 24)),
+            dma((ITERS, 2, 26)),
             dma((3,)),
         ],
         compiler_params=pltpu.CompilerParams(

time: 70.3 us -> 69.5 us (0.989)
    pallas_call x1, Pallas kernels: 68.2 us -> 67.5 us  [shards(): pl.pallas_call(kernel, out_shape=jax.ShapeDtypeStruct((2, COLS, ROWS), F3...]
where the time goes in v4:
time: 69.5 us; the launch traced here: 69.4 us
  Pallas kernels  67.5 us (97%)
  local copies, waits for them, and re-layouts  1.88 us (3%)
    pallas_call x1, Pallas kernels, shards(): pl.pallas_call(kernel, out_shape=jax.ShapeDtypeStruct((2, COLS, ROWS), F3...  67.5 us
    unnamed x1, local copies, waits for them, and re-layouts  1.88 us

profile of v4, /device:TPU:1, one launch (start us, length us, event | category | flops | bytes accessed | tf_op | source)
XLA Modules:
  0.0 69.4 jit_solution(17685440282387525987)
XLA Ops:
  0.0 67.5 %shard_map.37 = f32[2,128,512]{2,1,0:T(8,128)} custom-call(f32[2,128,512]{2,1,0:T(8,128)} %bitcast.5, f32[32,32]{1,0:T(8,128)} %ham_hbm.1, f32[32,32]{1,0:T(8,128)} %inter_hbm.1), custom_call_target="tpu_custom_call" | custom-call | flops 1610612736 | bytes 4194304 | tf_op jit(solution)/shard_map/pallas_call | solution.py:512
  67.5 1.9 %copy.6 = f32[2,8,1,16,512]{4,3,2,1,0:T(8,128)} copy(f32[2,8,1,16,512]{4,3,2,1,0:T(8,128)} %bitcast.4) | data formatting | bytes 1048576

commit v5 on v4

--- a/solution.py
+++ b/solution.py
@@ -37,12 +37,10 @@
 
 def kernel(
     green_hbm,
-    ham_hbm,
-    inter_hbm,
+    orbital_hbm,
     out_ref,
     green_ref,
-    ham_ref,
-    inter_ref,
+    orbital_ref,
     rounded,
     previous,
     earliest,
@@ -91,7 +89,7 @@
     inputs = [
         pltpu.make_async_copy(src, dst, input_sem.at[n])
         for n, (src, dst) in enumerate(
-            ((green_hbm, green_ref), (ham_hbm, ham_ref), (inter_hbm, inter_ref))
+            ((green_hbm, green_ref), (orbital_hbm, orbital_ref))
         )
     ]
     for copy in inputs:
@@ -383,14 +381,14 @@
                 )
 
     def prepare():
-        squared = inter_ref[...] * inter_ref[...]
+        squared = orbital_ref[1] * orbital_ref[1]
         pick = (iota((STRIPE, NO), 1) == core * STRIPE + iota((STRIPE, NO), 0)).astype(F32)
         picked = exact_dot(pick, squared, ((1,), (1,)))
         spread = (lax.rem(iota((NO, ROWS), 1), NO) == iota((NO, ROWS), 0)).astype(F32)
         weights[...] = exact_dot(picked, spread)
         tall = (lax.rem(iota((128, NO), 0), NO) == iota((128, NO), 1)).astype(F32)
         wide = (lax.rem(iota((NO, 128), 1), NO) == iota((NO, 128), 0)).astype(F32)
-        across = exact_dot(exact_dot(tall, ham_ref[...], ((1,), (1,))), wide)
+        across = exact_dot(exact_dot(tall, orbital_ref[0], ((1,), (1,))), wide)
         same = iota((128, 128), 0) // NO == iota((128, 128), 1) // NO
         blocked[...] = jnp.where(same, across, 0.0)
 
@@ -512,12 +510,11 @@
     result = pl.pallas_call(
         kernel,
         out_shape=jax.ShapeDtypeStruct((2, COLS, ROWS), F32),
-        in_specs=[pl.BlockSpec(memory_space=pltpu.HBM)] * 3,
+        in_specs=[pl.BlockSpec(memory_space=pltpu.HBM)] * 2,
         out_specs=whole,
         scratch_shapes=[
             pltpu.VMEM((2, COLS, ROWS), F32),
-            pltpu.VMEM((NO, NO), F32),
-            pltpu.VMEM((NO, NO), F32),
+            pltpu.VMEM((2, NO, NO), F32),
             pltpu.VMEM((ITERS, 2 * COLS, ROWS), BF16),
             pltpu.VMEM((ITERS, 2 * COLS, ROWS), BF16),
             pltpu.VMEM((ITERS, 2 * COLS, ROWS), BF16),
@@ -541,15 +538,15 @@
             dma((ITERS, 3)),
             dma((ITERS,)),
             dma((ITERS, 2, 26)),
-            dma((3,)),
+            dma((2,)),
         ],
         compiler_params=pltpu.CompilerParams(
-            collective_id=0, has_side_effects=True, vmem_limit_bytes=63 * 2**20 + 900000
+            collective_id=0, has_side_effects=True, vmem_limit_bytes=53 * 2**20 + 2**18
         ),
         cost_estimate=pl.CostEstimate(
             flops=ITERS * 8 * COLS * 1536 * ROWS, bytes_accessed=4 * 2**20, transcendentals=0
         ),
-    )(green.reshape(2, COLS, ROWS), hamiltonian, interaction)
+    )(green.reshape(2, COLS, ROWS), jnp.stack([hamiltonian, interaction]))
     return result.reshape(shape)
 
 

time: 69.5 us -> 68.6 us (0.987)
  local copies, waits for them, and re-layouts: 1.88 us -> 0.8 us
  other arithmetic: 0 us -> 0.74 us
  Pallas kernels: 67.5 us -> 66.8 us
    unnamed x1, local copies, waits for them, and re-layouts: 1.88 us -> 0.8 us
    another operation x0 -> x1, other arithmetic: none -> 0.74 us  [shards(): jnp.stack([hamiltonian, interaction])]
    pallas_call x1, Pallas kernels: 67.5 us -> 66.8 us  [shards(): pl.pallas_call(kernel, out_shape=jax.ShapeDtypeStruct((2, COLS, ROWS), F3...]
where the time goes in v5:
time: 68.6 us; the launch traced here: 68.3 us
  Pallas kernels  66.8 us (97%)
  local copies, waits for them, and re-layouts  0.8 us (1%)
  other arithmetic  0.74 us (1%)
    pallas_call x1, Pallas kernels, shards(): pl.pallas_call(kernel, out_shape=jax.ShapeDtypeStruct((2, COLS, ROWS), F3...  66.8 us

profile of v5, /device:TPU:1, one launch (start us, length us, event | category | flops | bytes accessed | tf_op | source)
XLA Modules:
  0.0 68.3 jit_solution(17752253923863213647)
XLA Ops:
  0.0 0.7 %pad_maximum_fusion.orbital_hbm = f32[2,32,32]{2,1,0:T(8,128)S(1)} fusion(f32[1,32,32]{2,1,0:T(8,128)} %bitcast.7, f32[1,32,32]{2,1,0:T(8,128)} %bitcast.8), kind=kLoop, calls=%fused_computation | loop fusion | flops 2048 | bytes 16384 | tf_op jit(solution)/shard_map/stack | solution.py:549
  0.7 66.8 %shard_map.37 = f32[2,128,512]{2,1,0:T(8,128)S(1)} custom-call(f32[2,128,512]{2,1,0:T(8,128)} %bitcast.9, f32[2,32,32]{2,1,0:T(8,128)S(1)} %pad_maximum_fusion.orbital_hbm), custom_call_target="tpu_custom_call" | custom-call | flops 1610612736 | bytes 4194304 | tf_op jit(solution)/shard_map/pallas_call | solution.py:510
  67.5 0.8 %copy.6 = f32[2,8,1,16,512]{4,3,2,1,0:T(8,128)} copy(f32[2,8,1,16,512]{4,3,2,1,0:T(8,128)S(1)} %bitcast.6) | data formatting | bytes 1048576

commit v6 on v5

--- a/solution.py
+++ b/solution.py
@@ -422,11 +422,11 @@
         if it == 0:
             prepare()
         lefts(it, 0, rounded, None)
+        hamilton_term(state)
         for copy in stages:
             copy.wait_recv()
         build_mirror(it)
         start_rows(1)
-        hamilton_term(state)
         for k in (0, 2):
             wait_bytes(mirror_bytes(mirror_in, it, k), mirror_recv.at[it, k])
             flip(it, k)

time: 68.6 us -> 68.6 us (level)
  no operation moved by 1% of the time
where the time goes in v6:
time: 68.6 us; the launch traced here: 68.3 us
  Pallas kernels  66.8 us (97%)
  local copies, waits for them, and re-layouts  0.8 us (1%)
  other arithmetic  0.74 us (1%)
    pallas_call x1, Pallas kernels, shards(): pl.pallas_call(kernel, out_shape=jax.ShapeDtypeStruct((2, COLS, ROWS), F3...  66.8 us

profile of v6, /device:TPU:1, one launch (start us, length us, event | category | flops | bytes accessed | tf_op | source)
XLA Modules:
  0.0 68.3 jit_solution(10190334793236894696)
XLA Ops:
  0.0 0.7 %pad_maximum_fusion.orbital_hbm = f32[2,32,32]{2,1,0:T(8,128)S(1)} fusion(f32[1,32,32]{2,1,0:T(8,128)} %bitcast.7, f32[1,32,32]{2,1,0:T(8,128)} %bitcast.8), kind=kLoop, calls=%fused_computation | loop fusion | flops 2048 | bytes 16384 | tf_op jit(solution)/shard_map/stack | solution.py:549
  0.7 66.8 %shard_map.37 = f32[2,128,512]{2,1,0:T(8,128)S(1)} custom-call(f32[2,128,512]{2,1,0:T(8,128)} %bitcast.9, f32[2,32,32]{2,1,0:T(8,128)S(1)} %pad_maximum_fusion.orbital_hbm), custom_call_target="tpu_custom_call" | custom-call | flops 1610612736 | bytes 4194304 | tf_op jit(solution)/shard_map/pallas_call | solution.py:510
  67.5 0.8 %copy.6 = f32[2,8,1,16,512]{4,3,2,1,0:T(8,128)} copy(f32[2,8,1,16,512]{4,3,2,1,0:T(8,128)S(1)} %bitcast.6) | data formatting | bytes 1048576
